TPU v7x, 32 devices: a whole 2x2x4 slice. The times are simulated.
32 devices in a mesh: grp: 2 (over y), space: 4 (over z), mem: 4 (over x, core).
Axes of the slice: x: 2, y: 2, z: 4, core: 2. Of those that a mesh axis runs over, the one named last changes fastest.
Arguments:
- starting_states: bfloat16 [8, 100, 4096], P(('grp', 'mem'), None, 'space'), parts along dimension 0, may hold values from -12 to 12
- observed: bfloat16 [200, 4096], P('grp', 'space'), parts along dimension 0, may hold values from -12 to 12
- mesh_feat: bfloat16 [512, 512], P('space'), may hold values from -6 to 6
- enc_send: int32 [4, 4, 128], P('space'), may hold values from 0 to 1023
- enc_edges: int32 [512, 16], P('space'), may hold values from 0 to 511, as said below
- dec_send: int32 [4, 4, 32], P('space'), may hold values from 0 to 127
- dec_edges: int32 [4096, 3], P('space'), may hold values from 0 to 127, as said below
- w_in: bfloat16 [100, 512], replicated, may hold values from -0.625 to 0.625
- w_src: bfloat16 [512, 512], replicated, may hold values from -0.25 to 0.25
- w_dst: bfloat16 [512, 512], replicated, may hold values from -0.25 to 0.25
- w_enc: bfloat16 [512, 512], replicated, may hold values from -0.25 to 0.25
- w_msg: bfloat16 [512, 512], replicated, may hold values from -0.25 to 0.25
- w_self: bfloat16 [512, 512], replicated, may hold values from -0.25 to 0.25
- w_hid: bfloat16 [512, 512], replicated, may hold values from -0.25 to 0.25
- decoder_variable_matrix: bfloat16 [512, 100], replicated, may hold values from -0.25 to 0.25
Outputs:
- predicted_member_states: bfloat16 [8, 100, 4096], P(('grp', 'mem'), None, 'space'), parts along dimension 0
- energy_loss: float32 [2], P('grp'), parts along dimension 0
- grad_out: float32 [1024, 100], P('grp'), parts along dimension 0
- grad_msg: bfloat16 [1024, 512], P('grp'), parts along dimension 0
There are 2 independent parts, one for each index of `grp`. A program takes and returns all parts, laid end to end along the dimension named above; an argument that names none is the same for every part. Nothing has to cross between parts.
Inputs may be any that keep to these rules, and one draw needn't show every extreme that they name: `enc_send`: entry [s, d, t] is the row of the grid points of index s that fills slot t of what s sends to d; a slot may repeat a row. `dec_send`: entry [s, d, t] is the row of the mesh nodes of index s that fills slot t of what s sends to d; a slot may repeat a row. `enc_edges`: for the nodes held by index d of space, each entry is s * 128 + t for a slot t among the first slots that source s fills for d; every filled slot is named by some entry of d; each of the 1 sources with a refined region fills all 128 slots to every d, the last index of space fills all of them to index 0, the other pairs fewer. `dec_edges`: for the grid points held by index d of space, each entry is s * 32 + t for a slot t among the first slots that source s fills for d; every filled slot is named by some entry of d; each of the 1 indices with a refined region receives all 32 slots from every source, index 0 receives all of them from the last index of space, the other pairs fewer.
All inputs are finite; a program needn't handle non-finite values.
Results may differ from a plain program's by a relative error of at most 0.007.
Values may be sent and summed in bfloat16 or wider, within the bound.
A program may use at most 128 MiB of HBM per device.

v0:
```python
import math

import jax
import jax.numpy as jnp
from jax import lax
from jax.sharding import PartitionSpec as P


def silu_slope(argument):
    logistic = jax.nn.sigmoid(argument)
    return logistic * (1.0 + argument * (1.0 - logistic))


def square_sums(row_block, observed_part):

    def per_member(member):
        member_f = member.astype(jnp.float32)
        diff = member_f - observed_part
        apart = row_block.astype(jnp.float32) - member_f[None]
        return (jnp.sum(diff * diff), jnp.sum(apart * apart, axis=(1, 2)))

    return lax.map(per_member, row_block)


def loss_terms(error_sq, pair_sq, entries):
    member_total_number = error_sq.shape[0]
    errors = jnp.sqrt(error_sq / entries + 1e-06)
    spreads = jnp.sqrt(pair_sq / entries + 1e-06)
    apart_mask = 1.0 - jnp.eye(member_total_number, dtype=jnp.float32)
    energy_loss = jnp.mean(errors) - jnp.sum(apart_mask * spreads) / (
        2.0 * member_total_number * member_total_number
    )
    weights = apart_mask / (member_total_number * member_total_number * entries * spreads)
    return (errors, weights, energy_loss)


def members_state_derivative(
    row_block, member_index, observed_part, errors, weights, scale_factor, entries
):
    member_total_number = row_block.shape[0]
    member = lax.dynamic_index_in_dim(row_block, member_index, 0, keepdims=False).astype(
        jnp.float32
    )
    first = (member - observed_part) / (member_total_number * entries * errors[member_index])

    def add_other(other_member, pulled):
        other_field = lax.dynamic_index_in_dim(row_block, other_member, 0, keepdims=False).astype(
            jnp.float32
        )
        return pulled + weights[member_index, other_member] * (member - other_field)

    pulled = lax.fori_loop(0, member_total_number, add_other, jnp.zeros_like(member))
    return (scale_factor * (first - pulled)).astype(jnp.bfloat16)


def local(
    starting_states,
    observed,
    mesh_feat,
    enc_send,
    enc_edges,
    dec_send,
    dec_edges,
    w_in,
    w_src,
    w_dst,
    w_enc,
    w_msg,
    w_self,
    w_hid,
    decoder_variable_matrix,
):
    members_state_array = starting_states[0]
    spaces = lax.axis_size("space")
    member_total_number = lax.axis_size("mem")
    entries = members_state_array.shape[0] * members_state_array.shape[1] * spaces
    scale_factor = member_total_number * math.sqrt(entries)
    grid_latent = jax.nn.silu(
        jnp.einsum("vg,vh->gh", members_state_array, w_in, preferred_element_type=jnp.float32)
    ).astype(jnp.bfloat16)
    projected = jnp.dot(grid_latent, w_src, preferred_element_type=jnp.float32).astype(jnp.bfloat16)
    outgoing = jnp.take(projected, enc_send[0], axis=0)
    arrived = lax.all_to_all(outgoing, "space", split_axis=0, concat_axis=0, tiled=True)
    received = arrived.reshape(-1, arrived.shape[2])
    node_query = jnp.dot(mesh_feat, w_dst, preferred_element_type=jnp.float32).astype(jnp.bfloat16)
    neighbours = jnp.take(received, enc_edges, axis=0).astype(jnp.float32)
    aggregate = jnp.mean(
        jax.nn.silu(neighbours + node_query.astype(jnp.float32)[:, None, :]), axis=1
    ).astype(jnp.bfloat16)
    mesh_latent = (
        mesh_feat.astype(jnp.float32)
        + jnp.dot(aggregate, w_enc, preferred_element_type=jnp.float32)
    ).astype(jnp.bfloat16)
    outgoing_mesh = jnp.take(mesh_latent, dec_send[0], axis=0)
    arrived_mesh = lax.all_to_all(outgoing_mesh, "space", split_axis=0, concat_axis=0, tiled=True)
    received_mesh = arrived_mesh.reshape(-1, arrived_mesh.shape[2])
    message = jnp.dot(received_mesh, w_msg, preferred_element_type=jnp.float32).astype(jnp.bfloat16)
    self_term = jnp.dot(grid_latent, w_self, preferred_element_type=jnp.float32)
    decoder_in = jnp.take(message, dec_edges, axis=0).astype(jnp.float32) + self_term[:, None, :]
    updated = (grid_latent.astype(jnp.float32) + jnp.mean(jax.nn.silu(decoder_in), axis=1)).astype(
        jnp.bfloat16
    )
    hidden_pre = jnp.dot(updated, w_hid, preferred_element_type=jnp.float32)
    inner_layer_response = jax.nn.silu(hidden_pre).astype(jnp.bfloat16)
    increment = jnp.einsum(
        "gh,hv->vg",
        inner_layer_response,
        decoder_variable_matrix,
        preferred_element_type=jnp.float32,
    )
    predicted_member_states = (members_state_array.astype(jnp.float32) + increment).astype(
        jnp.bfloat16
    )[None]
    ensemble = lax.all_gather(predicted_member_states, "mem", axis=0, tiled=True)
    observed_f = observed.astype(jnp.float32)
    error_sq, pair_sq = square_sums(ensemble, observed_f)
    error_sq, pair_sq = lax.psum((error_sq, pair_sq), "space")
    errors, weights, energy_loss = loss_terms(error_sq, pair_sq, entries)
    predicted_state_derivative = members_state_derivative(
        ensemble, lax.axis_index("mem"), observed_f, errors, weights, scale_factor, entries
    )
    part_out = jnp.einsum(
        "fu,sf->us",
        inner_layer_response,
        predicted_state_derivative,
        preferred_element_type=jnp.float32,
    )
    hidden_gradient = jnp.einsum(
        "tm,lt->ml",
        predicted_state_derivative,
        decoder_variable_matrix,
        preferred_element_type=jnp.float32,
    )
    pre_grad = (hidden_gradient * silu_slope(hidden_pre)).astype(jnp.bfloat16)
    updated_grad = jnp.einsum("gk,hk->gh", pre_grad, w_hid, preferred_element_type=jnp.float32)
    edge_grad = updated_grad[:, None, :] * silu_slope(decoder_in) / dec_edges.shape[1]
    message_grad = jax.ops.segment_sum(
        edge_grad.reshape(-1, edge_grad.shape[2]),
        dec_edges.reshape(-1),
        num_segments=message.shape[0],
    ).astype(jnp.bfloat16)
    part_msg = jnp.einsum(
        "rh,rk->hk", received_mesh, message_grad, preferred_element_type=jnp.float32
    )
    grad_out, grad_msg = lax.psum((part_out, part_msg), ("space", "mem"))
    return (
        predicted_member_states,
        jnp.reshape(energy_loss, (1,)),
        grad_out,
        grad_msg.astype(jnp.bfloat16),
    )


def solution(mesh):
    in_specs = (
        P(("grp", "mem"), None, "space"),
        P("grp", "space"),
        P("space", None),
        P("space", None, None),
        P("space", None),
        P("space", None, None),
        P("space", None),
        P(),
        P(),
        P(),
        P(),
        P(),
        P(),
        P(),
        P(),
    )
    out_specs = (P(("grp", "mem"), None, "space"), P("grp"), P("grp", None), P("grp", None))
    return jax.shard_map(local, mesh=mesh, in_specs=in_specs, out_specs=out_specs, check_vma=False)
```

profile of v0, /device:TPU:0, one launch (start us, length us, event | category | flops | bytes accessed | tf_op | source)
XLA Modules:
  0.0 263.8 jit_solution(2715755651103815272)
XLA Ops:
  7.2 0.7 compare_and_fusion.2
  8.6 1.8 multiply_convert_fusion.2
  10.4 1.0 copy-done.3
  12.2 2.0 gather_fusion
  14.2 0.9 broadcast_select_fusion
  15.1 6.3 %all-to-all-start = ((bf16[4,128,512]{2,1,0:T(8,128)(2,1)}), bf16[4,128,512]{2,1,0:T(8,128)(2,1)S(1)}, u32[]{:S(2)}, u32[]{:S(2)}) async-start(bf16[4,128,512]{2,1,0:T(8,128)(2,1)} %broadcast_select_fusion), calls=%async_computation | async-start | bytes 1048576 | tf_op jit(solution)/shard_map/all_to_all | solution.py:83
  23.4 0.8 convert_element_type.111
  24.4 0.9 reshape.143
  25.3 0.9 reshape.151
  26.2 2.1 fusion.39
  28.2 4.7 %add.200.clone = f32[1024,3,512]{2,1,0:T(4,128)} broadcast(f32[1024,512]{1,0:T(8,128)S(1)} %fusion.39), dimensions={0,2} | broadcast | bytes 8388608 | tf_op jit(solution)/shard_map/add | solution.py:99
  32.9 10.8 %add.210 = f32[3072,512]{1,0:T(8,128)} reshape(f32[1024,3,512]{2,1,0:T(4,128)} %add.200.clone) | data formatting | bytes 12582912 | tf_op jit(solution)/shard_map/add | solution.py:99
  44.8 1.3 fusion.25
  46.1 9.1 %gather_fusion.1 = bf16[2048,512]{1,0:T(8,128)(2,1)} fusion(bf16[512,512]{1,0:T(8,128)(2,1)S(1)} %bitcast.85, s32[2048]{0:T(1024)S(1)} %broadcast_clamp_fusion.1), kind=kCustom, calls=%fused_computation.1 | custom fusion | bytes 4202496 | tf_op jit(solution)/shard_map/jit(_take)/gather | solution.py:86
  55.2 3.1 %multiply_reduce_fusion.3 = f32[128,512]{1,0:T(8,128)S(1)} fusion(f32[128,512]{1,0:T(8,128)S(1)} %fusion.25, pred[128,16]{1,0:T(8,128)(4,1)} %copy.33, bf16[2048,512]{1,0:T(8,128)(2,1)} %gather_fusion.1), kind=kLoop, calls=%fused_computation.25 | loop fusion | flops 8323072 | bytes 2623488 | tf_op jit(solution)/shard_map/reduce_sum | solution.py:87
  58.3 1.3 fusion.24
  59.6 0.8 gather_fusion.2
  60.5 0.7 broadcast_select_fusion.1
  61.2 5.1 %all-to-all-start.1 = ((bf16[4,32,512]{2,1,0:T(8,128)(2,1)}), bf16[4,32,512]{2,1,0:T(8,128)(2,1)S(1)}, u32[]{:S(2)}, u32[]{:S(2)}) async-start(bf16[4,32,512]{2,1,0:T(8,128)(2,1)} %broadcast_select_fusion.1), calls=%async_computation.1 | async-start | bytes 262144 | tf_op jit(solution)/shard_map/all_to_all | solution.py:95
  66.4 5.9 %all-to-all-done.1 = bf16[4,32,512]{2,1,0:T(8,128)(2,1)S(1)} async-done(((bf16[4,32,512]{2,1,0:T(8,128)(2,1)}), bf16[4,32,512]{2,1,0:T(8,128)(2,1)S(1)}, u32[]{:S(2)}, u32[]{:S(2)}) %all-to-all-start.1) | async-done | bytes 131104 | tf_op jit(solution)/shard_map/all_to_all | solution.py:95
  72.3 1.3 convolution_convert_fusion.1
  73.5 13.2 %gather_fusion.3 = bf16[3072,512]{1,0:T(8,128)(2,1)} fusion(bf16[128,512]{1,0:T(8,128)(2,1)S(1)} %convolution_convert_fusion.1, s32[3072]{0:T(1024)S(1)} %broadcast_clamp_fusion), kind=kCustom, calls=%fused_computation.3 | custom fusion | bytes 6303744 | tf_op jit(solution)/shard_map/jit(_take)/gather | solution.py:99
  86.8 9.1 %reshape.142 = bf16[1024,3,512]{2,1,0:T(4,128)(2,1)} reshape(bf16[3072,512]{1,0:T(8,128)(2,1)} %gather_fusion.3) | data formatting | bytes 6291456 | tf_op jit(solution)/shard_map/jit(_take)/gather | solution.py:99
  95.9 4.9 %multiply_reduce_fusion.2 = f32[1024,512]{1,0:T(8,128)S(1)} fusion(bf16[1024,3,512]{2,1,0:T(4,128)(2,1)} %reshape.142, f32[1024,512]{1,0:T(8,128)S(1)} %fusion.39, pred[1024,3]{0,1:T(4,128)(4,1)S(1)} %compare_and_fusion), kind=kLoop, calls=%fused_computation.24 | loop fusion | flops 12058624 | bytes 7343104 | tf_op jit(solution)/shard_map/reduce_sum | solution.py:100
  100.8 2.2 multiply_convert_fusion.1
  103.5 9.1 %all-gather.1 = bf16[4,100,1024]{2,1,0:T(8,128)(2,1)S(1)} all-gather(bf16[1,100,1024]{2,1,0:T(8,128)(2,1)S(1)} %fusion.23), channel_id=2, replica_groups=mesh['grp'=2,'space'=4,'mem'=4] {'mem'}, dimensions={0}, use_global_device_ids=true | all-gather | bytes 1024000 | tf_op jit(solution)/shard_map/all_gather | solution.py:114
  112.7 7.7 %while.28 = (s32[]{:T(128)}, f32[4]{0:T(128)S(1)}, f32[4,4]{1,0:T(4,128)S(1)}, bf16[4,100,1024]{2,1,0:T(8,128)(2,1)S(1)}, f32[100,1024]{1,0:T(8,128)S(1)}, /*index=5*/s32[]{:T(128)}, s32[]{:T(128)}) while((s32[]{:T(128)}, f32[4]{0:T(128)S(1)}, f32[4,4]{1,0:T(4,128)S(1)}, bf16[4,100,1024]{2,1,0:T(8,128)(2,1)S(1)}, f32[100,1024]{1,0:T(8,128)S(1)}, ...), condition=%wide.region_5.6_spmd, body=%wide.region_2.5_spmd.sunk | while | flops 2150397 | bytes 2457761 | solution.py:22
  112.7 0.7 multiply_reduce_fusion.7
  113.4 0.8 dynamic_update_slice.10
  115.3 0.8 dynamic_update_slice.10
  116.5 0.7 multiply_reduce_fusion.7
  117.2 0.8 dynamic_update_slice.10
  118.4 0.7 multiply_reduce_fusion.7
  119.2 0.8 dynamic_update_slice.10
  120.4 9.8 %all-reduce = (f32[4]{0:T(128)S(1)}, f32[4,4]{1,0:T(4,128)S(1)}) all-reduce(f32[4]{0:T(128)S(1)} %get-tuple-element.183, f32[4,4]{1,0:T(4,128)S(1)} %get-tuple-element.184), channel_id=1, replica_groups=mesh['grp'=2,'space'=4,'mem'=4] {'space'}, use_global_device_ids=true, to_apply=%region_6.7 | all-reduce | flops 20 | bytes 160 | tf_op jit(solution)/shard_map/psum | solution.py:117
  132.0 5.7 %while.29 = (s32[]{:T(128)}, f32[100,1024]{1,0:T(8,128)S(1)}, f32[4,4]{1,0:T(4,128)S(1)}, s32[]{:T(128)}, bf16[4,100,1024]{2,1,0:T(8,128)(2,1)S(1)}, /*index=5*/f32[100,1024]{1,0:T(8,128)S(1)}, s32[]{:T(128)}, s32[]{:T(128)}) while((s32[]{:T(128)}, f32[100,1024]{1,0:T(8,128)S(1)}, f32[4,4]{1,0:T(4,128)S(1)}, s32[]{:T(128)}, ...), condition=%wide.region_11.12_spmd.clone, body=%wide.region_10.11_spmd.clone.sunk | while | flops 512003 | bytes 1433723 | solution.py:52
  132.6 0.8 fusion.61
  134.0 0.8 fusion.61
  135.5 0.8 fusion.61
  136.9 0.8 fusion.61
  138.4 1.0 multiply_convert_fusion.3
  139.4 1.0 fusion.40
  140.4 3.1 %fusion.20 = f32[1024,512]{1,0:T(8,128)S(1)} fusion(bf16[512,512]{1,0:T(8,128)(2,1)S(1)} %copy-done, f32[1024,512]{1,0:T(8,128)} %get-tuple-element.236, bf16[100,1024]{1,0:T(8,128)(2,1)} %copy-done.7, bf16[512,100]{0,1:T(8,128)(2,1)S(1)} %copy-done.11), kind=kOutput, calls=%fused_computation.38 | convolution fusion | flops 646447104 | bytes 5025792 | tf_op jit(solution)/shard_map/gk,hk->gh/dot_general | solution.py:135
  143.5 4.7 %mul.90 = f32[1024,3,512]{2,1,0:T(4,128)} broadcast(f32[1024,512]{1,0:T(8,128)S(1)} %fusion.20), dimensions={0,2} | broadcast | bytes 8388608 | tf_op jit(solution)/shard_map/mul | solution.py:136
  148.2 10.7 %mul.91 = f32[3072,512]{1,0:T(8,128)} reshape(f32[1024,3,512]{2,1,0:T(4,128)} %mul.90) | data formatting | bytes 12582912 | tf_op jit(solution)/shard_map/mul | solution.py:136
  158.9 23.8 %scatter_custom_fusion = f32[128,512]{1,0:T(8,128)S(1)} fusion(s32[3072]{0:T(1024)} %reshape.151, f32[3072,512]{1,0:T(8,128)} %mul.91, f32[3072,512]{1,0:T(8,128)} %add.210, f32[]{:T(128)} %constant.151.clone.1, bf16[3072,512]{1,0:T(8,128)(2,1)} %gather_fusion.3, f32[]{:T(128)} %constant.140.clone.1, pred[3072]{0:T(1024)(128)(4,1)S(1)} %broadcast_in_dim.84, ...), kind=kCustom, calls=%fused_computation.11 | custom fusion | flops 20447232 | bytes 15995904 | tf_op jit(solution)/shard_map/scatter-add | solution.py:137
  183.0 69.9 %all-reduce.5 = bf16[512,512]{1,0:T(8,128)(2,1)} all-reduce(f32[512,512]{1,0:T(8,128)S(1)} %fusion.30), channel_id=1, replica_groups=mesh['grp'=2,'space'=4,'mem'=4] {'space','mem'}, use_global_device_ids=true, to_apply=%region_14.15 | all-reduce | flops 262144 | bytes 1572864 | tf_op jit(solution)/shard_map/psum | solution.py:145
  254.2 1.6 copy.64
  (89 shorter events, 12.2 us)
Async XLA Ops:
  7.2 93.6 %copy-start = (bf16[512,512]{1,0:T(8,128)(2,1)S(1)}, bf16[512,512]{1,0:T(8,128)(2,1)}, u32[]{:S(2)}) copy-start(bf16[512,512]{1,0:T(8,128)(2,1)} %param.32) | copy-start | bytes 1572868
  8.6 2.8 %copy-start.19 = (bf16[512,512]{1,0:T(8,128)(2,1)S(1)}, bf16[512,512]{1,0:T(8,128)(2,1)}, u32[]{:S(2)}) copy-start(bf16[512,512]{1,0:T(8,128)(2,1)} %param.27) | copy-start | bytes 1572868
  10.4 1.0 copy-start.3
  12.1 9.3 %copy-start.13 = (s32[128,16]{0,1:T(8,128)S(1)}, s32[128,16]{0,1:T(8,128)}, u32[]{:S(2)}) copy-start(s32[128,16]{0,1:T(8,128)} %param.23) | copy-start | bytes 24580
  12.1 9.3 %copy-start.10 = (s32[1024,3]{0,1:T(4,128)S(1)}, s32[1024,3]{0,1:T(4,128)}, u32[]{:S(2)}) copy-start(s32[1024,3]{0,1:T(4,128)} %param.25) | copy-start | bytes 36868
  12.2 9.6 %copy-start.15 = (s32[1,4,32]{2,1,0:T(4,128)S(1)}, s32[1,4,32]{2,1,0:T(4,128)}, u32[]{:S(2)}) copy-start(s32[1,4,32]{2,1,0:T(4,128)} %param.24) | copy-start | bytes 1540
  12.2 11.2 %copy-start.5 = (bf16[100,1024]{1,0:T(8,128)(2,1)S(1)}, bf16[100,1024]{1,0:T(8,128)(2,1)}, u32[]{:S(2)}) copy-start(bf16[100,1024]{1,0:T(8,128)(2,1)} %param.20) | copy-start | bytes 614404
  15.1 31.0 %all-to-all-start = ((bf16[4,128,512]{2,1,0:T(8,128)(2,1)}), bf16[4,128,512]{2,1,0:T(8,128)(2,1)S(1)}, u32[]{:S(2)}, u32[]{:S(2)}) async-start(bf16[4,128,512]{2,1,0:T(8,128)(2,1)} %broadcast_select_fusion), calls=%async_computation | async-start | bytes 1048576 | tf_op jit(solution)/shard_map/all_to_all | solution.py:83
  32.9 11.9 %copy-start.8 = (bf16[128,512]{1,0:T(8,128)(2,1)S(1)}, bf16[128,512]{1,0:T(8,128)(2,1)}, u32[]{:S(2)}) copy-start(bf16[128,512]{1,0:T(8,128)(2,1)} %param.21) | copy-start | bytes 393220
  55.2 4.4 %copy-start.14 = (s32[1024]{0:T(1024)S(1)}, s32[1024]{0:T(1024)}, u32[]{:S(2)}) copy-start(s32[1024]{0:T(1024)} %pad_clamp_fusion) | copy-start | bytes 12292
  55.2 5.3 %copy-start.16 = (pred[4,32]{1,0:T(4,128)(4,1)S(1)}, pred[4,32]{1,0:T(4,128)(4,1)}, u32[]{:S(2)}) copy-start(pred[4,32]{1,0:T(4,128)(4,1)} %compare_and_fusion.3) | copy-start | bytes 388
  55.2 11.1 %copy-start.12 = (s32[3072]{0:T(1024)S(1)}, s32[3072]{0:T(1024)}, u32[]{:S(2)}) copy-start(s32[3072]{0:T(1024)} %reshape.143) | copy-start | bytes 36868
  61.2 11.0 %all-to-all-start.1 = ((bf16[4,32,512]{2,1,0:T(8,128)(2,1)}), bf16[4,32,512]{2,1,0:T(8,128)(2,1)S(1)}, u32[]{:S(2)}, u32[]{:S(2)}) async-start(bf16[4,32,512]{2,1,0:T(8,128)(2,1)} %broadcast_select_fusion.1), calls=%async_computation.1 | async-start | bytes 262144 | tf_op jit(solution)/shard_map/all_to_all | solution.py:95
  66.3 187.9 %all-reduce.4.cloned.1.call-start = ((), (), s32[]{:S(2)}) async-start(), calls=%async_computation.2 | async-start | bytes 425984 | tf_op jit(solution)/shard_map/psum | solution.py:145
  95.9 4.9 %copy-start.4 = (bf16[1024,512]{1,0:T(8,128)(2,1)S(1)}, bf16[1024,512]{1,0:T(8,128)(2,1)}, u32[]{:S(2)}) copy-start(bf16[1024,512]{1,0:T(8,128)(2,1)} %copy-done.3) | copy-start | bytes 3145732
  100.7 2.3 copy-start.9
  100.8 2.3 copy-start.11
  100.8 11.9 %copy-start.1 = (f32[100,1024]{1,0:T(8,128)S(1)}, f32[100,1024]{1,0:T(8,128)}, u32[]{:S(2)}) copy-start(f32[100,1024]{1,0:T(8,128)} %convert_element_type.111) | copy-start | bytes 1228804
  100.8 11.9 %copy-start.17 = (f32[4,4]{1,0:T(4,128)S(1)}, f32[4,4]{1,0:T(4,128)}, u32[]{:S(2)}) copy-start(f32[4,4]{1,0:T(4,128)} %custom-call.10) | copy-start | bytes 196
  100.8 11.9 %copy-start.18 = (f32[4]{0:T(128)S(1)}, f32[4]{0:T(128)}, u32[]{:S(2)}) copy-start(f32[4]{0:T(128)} %custom-call.9) | copy-start | bytes 52
  103.5 9.1 %copy-start.6 = (bf16[1,100,1024]{2,1,0:T(8,128)(2,1)}, bf16[1,100,1024]{2,1,0:T(8,128)(2,1)S(1)}, u32[]{:S(2)}) copy-start(bf16[1,100,1024]{2,1,0:T(8,128)(2,1)S(1)} %fusion.23) | copy-start | bytes 614404
  112.7 19.3 %copy-start.2 = (f32[100,1024]{1,0:T(8,128)S(1)}, f32[100,1024]{1,0:T(8,128)}, u32[]{:S(2)}) copy-start(f32[100,1024]{1,0:T(8,128)} %custom-call) | copy-start | bytes 1228804
  139.4 1.0 copy-start.7
Sparse Core Ops, SparseCore 0:
  143.6 85.6 all-reduce.3
where the time goes:
time: 265 us; the launch traced here: 264 us
  blocking collectives  88.8 us (34%)
  local copies, waits for them, and re-layouts  77.7 us (29%)
  other arithmetic  46.9 us (18%)
  between operations  17.4 us (7%)
  matrix products  15.4 us (6%)
  starting transfers between devices  11.4 us (4%)
  waiting for transfers between devices  5.95 us (2%)
    psum x1, blocking collectives, local(): grad_out, grad_msg = lax.psum((part_out, part_msg), ('space', 'mem'))  69.9 us
    scatter-add x1, other arithmetic, local(): jax.ops.segment_sum(edge_grad.reshape(-1, edge_grad.shape[2]), dec_edges....  23.8 us
    gather x2, local copies, waits for them, and re-layouts, local(): jnp.take(message, dec_edges, axis=0).astype(jnp.float32)  22.3 us
    add x2, local copies, waits for them, and re-layouts, local(): jnp.take(message, dec_edges, axis=0).astype(jnp.float32)  15.4 us
    mul x2, local copies, waits for them, and re-layouts, local(): updated_grad[:, None, :] * silu_slope(decoder_in) / dec_edges.shape[1]  15.4 us
    psum x1, blocking collectives, local(): error_sq, pair_sq = lax.psum((error_sq, pair_sq), 'space')  9.78 us
    gather x1, local copies, waits for them, and re-layouts, local(): neighbours = jnp.take(received, enc_edges, axis=0).astype(jnp.float32)  9.14 us
    all_gather x1, blocking collectives, local(): lax.all_gather(predicted_member_states, 'mem', axis=0, tiled=True)  9.13 us
  transfers between devices with their start and end apart: 3, of which 1 were waited for; matrix products, arithmetic and copies ran while one was open for 24% of the time, Pallas kernels for 0%

commit v1 on v0

--- a/solution.py
+++ b/solution.py
@@ -1,9 +1,444 @@
+import functools
 import math
 
 import jax
 import jax.numpy as jnp
 from jax import lax
+from jax.experimental import pallas as pl
+from jax.experimental.pallas import tpu as pltpu
 from jax.sharding import PartitionSpec as P
+
+MESH = pl.DeviceIdType.MESH
+F32 = jnp.float32
+BF16 = jnp.bfloat16
+ROWS = 112
+CHUNKS = 4
+
+
+def dot(a, b, contract=(1, 0)):
+    return lax.dot_general(
+        a, b, (((contract[0],), (contract[1],)), ((), ())), preferred_element_type=F32
+    )
+
+
+def sigmoid(v):
+    return 0.5 * jnp.tanh(0.5 * v) + 0.5
+
+
+def silu(v):
+    return v * sigmoid(v)
+
+
+def slope(v):
+    g = sigmoid(v)
+    return g * (1.0 + v * (1.0 - g))
+
+
+def one_hot(hit):
+    return jnp.where(hit, 1.0, 0.0).astype(BF16)
+
+
+def step_kernel(
+    spaces, members,
+    x_ref, obs_ref, feat_ref, esend_ref, eedge_ref, dsend_ref, dedge_ref, dedge_t_ref,
+    w_in_ref, w_src_ref, w_dst_ref, w_enc_ref, w_msg_ref, w_self_ref, w_hid_ref, dvm_t_ref,
+    pred_ref, loss_ref, gout_ref, gmsg_ref,
+    xp, obsp, winp, dvmp,
+    xs_send, xs_recv, gl, self_term, ehot, dhot, dhot_t, arr_gl, arr, nq,
+    ms_send, ma, dec_in, hid, act, ens, st, st_recv, loss_s, loss_r, fgs,
+    gos, gor, gs, gq, aall, at, q32, qb, q_recv, gq32, gq_recv, fin, gfin,
+    x_ss, x_rs, m_ss, m_rs, e_ss, e_rs, a_ss, a_rs, s_ss, s_rs, l_ss, l_rs,
+    o_ss, o_rs, g_ss, g_rs, zq_ss, zq_rs, zo_ss, zo_rs, c1_ss, c1_rs, d1_ss, d1_rs,
+    c2_ss, c2_rs, d2_ss, d2_rs,
+):
+    grp, sp, me = lax.axis_index("grp"), lax.axis_index("space"), lax.axis_index("mem")
+    varn, grid = obs_ref.shape
+    latent = w_src_ref.shape[0]
+    nodes = feat_ref.shape[0]
+    ecap, dcap = esend_ref.shape[2], dsend_ref.shape[2]
+    slots, dslots = spaces * ecap, spaces * dcap
+    k_enc, k_dec = eedge_ref.shape[1], dedge_ref.shape[1]
+    part = grid // CHUNKS
+    entries = varn * grid * spaces
+    quarter = latent // members
+    zrows = latent // spaces
+
+    def space_at(o):
+        return lax.rem(sp + o, spaces)
+
+    def mem_at(o):
+        return lax.rem(me + o, members)
+
+    def to_space(src, dst, ss, rs, o):
+        return pltpu.make_async_remote_copy(
+            src_ref=src, dst_ref=dst, send_sem=ss.at[o], recv_sem=rs.at[o],
+            device_id=(grp, space_at(o), me), device_id_type=MESH,
+        )
+
+    def to_mem(src, dst, ss, rs, o):
+        return pltpu.make_async_remote_copy(
+            src_ref=src, dst_ref=dst, send_sem=ss, recv_sem=rs,
+            device_id=(grp, sp, mem_at(o)), device_id_type=MESH,
+        )
+
+    barrier = pltpu.get_barrier_semaphore()
+    for o in range(1, spaces):
+        pl.semaphore_signal(barrier, inc=1, device_id=(grp, space_at(o), me), device_id_type=MESH)
+    for o in range(1, members):
+        pl.semaphore_signal(barrier, inc=1, device_id=(grp, sp, mem_at(o)), device_id_type=MESH)
+
+    xp[96:ROWS, :] = jnp.zeros((ROWS - 96, grid), BF16)
+    xp[0:varn, :] = x_ref[0]
+    winp[96:ROWS, :] = jnp.zeros((ROWS - 96, latent), BF16)
+    winp[0:varn, :] = w_in_ref[...]
+
+    grid_rows = lax.broadcasted_iota(jnp.int32, (grid, ecap), 0)
+    xs = []
+    waited = False
+    for o in list(range(1, spaces)) + [0]:
+        row = esend_ref[0, pl.ds(space_at(o), 1), :]
+        hot = one_hot(grid_rows == row)
+        picked = dot(xp[...], hot).astype(BF16)
+        if o == 0:
+            xs_recv[sp] = picked
+        else:
+            xs_send[o] = picked
+            if not waited:
+                pl.semaphore_wait(barrier, spaces + members - 2)
+                waited = True
+            copy = to_space(xs_send.at[o], xs_recv.at[sp], x_ss, x_rs, o)
+            copy.start()
+            xs.append(copy)
+
+    obsp[96:ROWS, :] = jnp.zeros((ROWS - 96, grid), BF16)
+    obsp[0:varn, :] = obs_ref[...]
+    dvmp[96:ROWS, :] = jnp.zeros((ROWS - 96, latent), BF16)
+    dvmp[0:varn, :] = dvm_t_ref[...]
+    nq[...] = dot(feat_ref[...], w_dst_ref[...]).astype(BF16).astype(F32)
+    slot_cols = lax.broadcasted_iota(jnp.int32, (nodes, slots), 1)
+    for k in range(k_enc):
+        ehot[k * nodes:(k + 1) * nodes, :] = one_hot(slot_cols == eedge_ref[:, k:k + 1])
+    for c in range(CHUNKS):
+        rows = slice(c * part, (c + 1) * part)
+        gl[rows, :] = silu(dot(xp[:, rows], winp[...], (0, 0))).astype(BF16)
+
+    for copy in xs:
+        copy.wait()
+    for s in range(spaces):
+        arr_gl[s * ecap:(s + 1) * ecap, :] = silu(dot(xs_recv[s], winp[...], (0, 0))).astype(BF16)
+    arr[...] = dot(arr_gl[...], w_src_ref[...]).astype(BF16)
+    total = jnp.zeros((nodes, latent), F32)
+    group = 4
+    for k in range(0, k_enc, group):
+        v = dot(ehot[k * nodes:(k + group) * nodes, :], arr[...])
+        for i in range(group):
+            total += silu(v[i * nodes:(i + 1) * nodes, :] + nq[...])
+    aggregate = (total * (1.0 / k_enc)).astype(BF16)
+    mesh_latent = (feat_ref[...].astype(F32) + dot(aggregate, w_enc_ref[...])).astype(BF16)
+
+    node_rows = lax.broadcasted_iota(jnp.int32, (nodes, dcap), 0)
+    ms = []
+    for o in list(range(1, spaces)) + [0]:
+        row = dsend_ref[0, pl.ds(space_at(o), 1), :]
+        picked = dot(one_hot(node_rows == row), mesh_latent, (0, 0)).astype(BF16)
+        if o == 0:
+            ma[sp] = picked
+        else:
+            ms_send[o] = picked
+            copy = to_space(ms_send.at[o], ma.at[sp], m_ss, m_rs, o)
+            copy.start()
+            ms.append(copy)
+    dcols = lax.broadcasted_iota(jnp.int32, (grid, dslots), 1)
+    drows = lax.broadcasted_iota(jnp.int32, (dslots, grid), 0)
+    for k in range(k_dec):
+        dhot[k] = one_hot(dcols == dedge_ref[:, k:k + 1])
+        dhot_t[k] = one_hot(drows == dedge_t_ref[k:k + 1, :])
+    for c in range(CHUNKS):
+        rows = slice(c * part, (c + 1) * part)
+        self_term[rows, :] = dot(gl[rows, :], w_self_ref[...])
+    for copy in ms:
+        copy.wait()
+
+    arrivals = ma[...].reshape(dslots, latent)
+    aall[0] = arrivals
+    message = dot(arrivals, w_msg_ref[...]).astype(BF16)
+    es = []
+    for c in range(CHUNKS):
+        rows = slice(c * part, (c + 1) * part)
+        acc = jnp.zeros((part, latent), F32)
+        own = self_term[rows, :]
+        for k in range(k_dec):
+            v = dot(dhot[k, rows, :], message) + own
+            dec_in[k, rows, :] = v
+            acc += silu(v)
+        updated = (gl[rows, :].astype(F32) + acc * (1.0 / k_dec)).astype(BF16)
+        pre = dot(updated, w_hid_ref[...])
+        hid[rows, :] = pre
+        response = silu(pre).astype(BF16)
+        act[rows, :] = response
+        increment = dot(dvmp[...], response, (1, 1))
+        predicted = (xp[:, rows].astype(F32) + increment).astype(BF16)
+        ens[0, c] = predicted
+        pred_ref[0, :, rows] = predicted[0:varn, :]
+        for o in range(1, members):
+            copy = to_mem(
+                ens.at[0, c], ens.at[members - o, c], e_ss.at[o, c], e_rs.at[o, c], o
+            )
+            copy.start()
+            es.append(copy)
+    as_ = []
+    for o in range(1, members):
+        copy = to_mem(aall.at[0], aall.at[members - o], a_ss.at[o], a_rs.at[o], o)
+        copy.start()
+        as_.append(copy)
+
+    for c in range(CHUNKS):
+        rows = slice(c * part, (c + 1) * part)
+        hid[rows, :] = slope(hid[rows, :])
+        for k in range(k_dec):
+            dec_in[k, rows, :] = slope(dec_in[k, rows, :]) * (1.0 / k_dec)
+
+    def folded(d):
+        d = (d * d).reshape(ROWS // 8, 8, part).sum(axis=0)
+        out = d[:, 0:128]
+        for i in range(1, part // 128):
+            out += d[:, i * 128:(i + 1) * 128]
+        return out
+
+    sums = [jnp.zeros((8, 128), F32) for _ in range(members)]
+    for copy in es:
+        copy.wait()
+    for c in range(CHUNKS):
+        rows = slice(c * part, (c + 1) * part)
+        mine = ens[0, c].astype(F32)
+        sums[0] += folded(mine - obsp[:, rows].astype(F32))
+        for j in range(1, members):
+            sums[j] += folded(mine - ens[j, c].astype(F32))
+    for j in range(members):
+        st[j] = sums[j]
+    ss = []
+    for o in range(1, spaces):
+        copy = to_space(st, st_recv.at[o], s_ss, s_rs, o)
+        copy.start()
+        ss.append(copy)
+    for copy in ss:
+        copy.wait()
+    tot = st[...]
+    for o in range(1, spaces):
+        tot += st_recv[o]
+    root = jnp.sqrt(jnp.sum(tot, axis=(1, 2), keepdims=True) / entries + 1e-06)
+    error = root[0]
+    my_loss = error / members
+    for j in range(1, members):
+        my_loss -= root[j] / (2.0 * members * members)
+    loss_s[...] = jnp.broadcast_to(my_loss, (8, 128))
+    ls = []
+    for o in range(1, members):
+        copy = to_mem(loss_s, loss_r.at[o], l_ss.at[o], l_rs.at[o], o)
+        copy.start()
+        ls.append(copy)
+    scale = members * math.sqrt(entries)
+    first = scale / (members * entries * error)
+    pulls = [scale / (members * members * entries * root[j]) for j in range(1, members)]
+
+    gout = jnp.zeros((ROWS, latent), F32)
+    for c in range(CHUNKS):
+        rows = slice(c * part, (c + 1) * part)
+        mine = ens[0, c].astype(F32)
+        fg = first * (mine - obsp[:, rows].astype(F32))
+        for j in range(1, members):
+            fg -= pulls[j - 1] * (mine - ens[j, c].astype(F32))
+        fg = fg.astype(BF16)
+        fgs[c] = fg
+        gout += dot(fg, act[rows, :])
+    for m in range(members):
+        gos[m, 0:ROWS, :] = gout[:, m * quarter:(m + 1) * quarter]
+        gos[m, ROWS:128, :] = jnp.zeros((128 - ROWS, quarter), F32)
+    os_ = []
+    for o in range(1, members):
+        copy = to_mem(gos.at[mem_at(o)], gor.at[o], o_ss.at[o], o_rs.at[o], o)
+        copy.start()
+        os_.append(copy)
+
+    mgrad = jnp.zeros((dslots, latent), F32)
+    for c in range(CHUNKS):
+        rows = slice(c * part, (c + 1) * part)
+        hgrad = dot(fgs[c], dvmp[...], (0, 0))
+        pre_grad = (hgrad * hid[rows, :]).astype(BF16)
+        ugrad = dot(pre_grad, w_hid_ref[...], (1, 1))
+        for k in range(k_dec):
+            edge = (ugrad * dec_in[k, rows, :]).astype(BF16)
+            mgrad += dot(dhot_t[k, :, rows], edge)
+    for m in range(members):
+        gs[m] = mgrad[:, m * quarter:(m + 1) * quarter].astype(BF16)
+    gsent = []
+    for o in range(1, members):
+        copy = to_mem(gs.at[mem_at(o)], gq.at[members - o], g_ss.at[o], g_rs.at[o], o)
+        copy.start()
+        gsent.append(copy)
+    gq[0] = gs[me]
+    for copy in as_:
+        copy.wait()
+    for j in range(members):
+        at[:, j * dslots:(j + 1) * dslots] = aall[j].astype(F32).T.astype(BF16)
+    for copy in os_:
+        copy.wait()
+    oq = gos[me]
+    for o in range(1, members):
+        oq += gor[o]
+    gq32[...] = oq.reshape(spaces, 128 // spaces, quarter)
+    zo = []
+    for o in range(1, spaces):
+        copy = to_space(gq32.at[space_at(o)], gq_recv.at[o], zo_ss, zo_rs, o)
+        copy.start()
+        zo.append(copy)
+    for copy in gsent:
+        copy.wait()
+    q = dot(at[...], gq[...].reshape(members * dslots, quarter)).reshape(spaces, zrows, quarter)
+    q32[...] = q
+    qb[...] = q.astype(BF16)
+    zq = []
+    for o in range(1, spaces):
+        copy = to_space(qb.at[space_at(o)], q_recv.at[o], zq_ss, zq_rs, o)
+        copy.start()
+        zq.append(copy)
+    for copy in zo:
+        copy.wait()
+    gsum = gq32[sp]
+    for o in range(1, spaces):
+        gsum += gq_recv[o]
+    gfin[me, sp] = gsum
+    d1 = []
+    for o in range(1, spaces):
+        copy = to_space(gfin.at[me, sp], gfin.at[me, sp], d1_ss, d1_rs, o)
+        copy.start()
+        d1.append(copy)
+    for copy in zq:
+        copy.wait()
+    r = q32[sp]
+    for o in range(1, spaces):
+        r += q_recv[o].astype(F32)
+    fin[me, sp] = r.astype(BF16)
+    c1 = []
+    for o in range(1, spaces):
+        copy = to_space(fin.at[me, sp], fin.at[me, sp], c1_ss, c1_rs, o)
+        copy.start()
+        c1.append(copy)
+    for copy in d1:
+        copy.wait()
+    d2 = []
+    for o in range(1, members):
+        copy = to_mem(gfin.at[me], gfin.at[me], d2_ss.at[o], d2_rs.at[o], o)
+        copy.start()
+        d2.append(copy)
+    for copy in c1:
+        copy.wait()
+    c2 = []
+    for o in range(1, members):
+        copy = to_mem(fin.at[me], fin.at[me], c2_ss.at[o], c2_rs.at[o], o)
+        copy.start()
+        c2.append(copy)
+    for copy in ls:
+        copy.wait()
+    all_loss = loss_s[...]
+    for o in range(1, members):
+        all_loss += loss_r[o]
+    loss_ref[0] = jnp.max(all_loss)
+    for copy in d2:
+        copy.wait()
+    for m in range(members):
+        block = gfin[m].reshape(128, quarter).T
+        gout_ref[m * quarter:(m + 1) * quarter, :] = block[:, 0:varn]
+    for copy in c2:
+        copy.wait()
+    for m in range(members):
+        gmsg_ref[:, m * quarter:(m + 1) * quarter] = fin[m].reshape(latent, quarter)
+
+
+def fused(
+    starting_states, observed, mesh_feat, enc_send, enc_edges, dec_send, dec_edges,
+    w_in, w_src, w_dst, w_enc, w_msg, w_self, w_hid, decoder_variable_matrix,
+):
+    spaces, members = lax.axis_size("space"), lax.axis_size("mem")
+    varn, grid = observed.shape
+    latent = w_src.shape[0]
+    nodes = mesh_feat.shape[0]
+    ecap, dcap = enc_send.shape[2], dec_send.shape[2]
+    slots, dslots = spaces * ecap, spaces * dcap
+    k_enc, k_dec = enc_edges.shape[1], dec_edges.shape[1]
+    part = grid // CHUNKS
+    quarter = latent // members
+    zrows = latent // spaces
+    vmem = pltpu.VMEM
+    scratch = [
+        vmem((ROWS, grid), BF16), vmem((ROWS, grid), BF16),
+        vmem((ROWS, latent), BF16), vmem((ROWS, latent), BF16),
+        vmem((spaces, ROWS, ecap), BF16), vmem((spaces, ROWS, ecap), BF16),
+        vmem((grid, latent), BF16), vmem((grid, latent), F32),
+        vmem((k_enc * nodes, slots), BF16),
+        vmem((k_dec, grid, dslots), BF16), vmem((k_dec, dslots, grid), BF16),
+        vmem((slots, latent), BF16), vmem((slots, latent), BF16), vmem((nodes, latent), F32),
+        vmem((spaces, dcap, latent), BF16), vmem((spaces, dcap, latent), BF16),
+        vmem((k_dec, grid, latent), F32), vmem((grid, latent), F32), vmem((grid, latent), BF16),
+        vmem((members, CHUNKS, ROWS, part), BF16),
+        vmem((members, 8, 128), F32), vmem((spaces, members, 8, 128), F32),
+        vmem((8, 128), F32), vmem((members, 8, 128), F32),
+        vmem((CHUNKS, ROWS, part), BF16),
+        vmem((members, 128, quarter), F32), vmem((members, 128, quarter), F32),
+        vmem((members, dslots, quarter), BF16), vmem((members, dslots, quarter), BF16),
+        vmem((members, dslots, latent), BF16), vmem((latent, members * dslots), BF16),
+        vmem((spaces, zrows, quarter), F32), vmem((spaces, zrows, quarter), BF16),
+        vmem((spaces, zrows, quarter), BF16),
+        vmem((spaces, 128 // spaces, quarter), F32), vmem((spaces, 128 // spaces, quarter), F32),
+        vmem((members, spaces, zrows, quarter), BF16),
+        vmem((members, spaces, 128 // spaces, quarter), F32),
+    ]
+    dma = pltpu.SemaphoreType.DMA
+    scratch += [dma((spaces,))] * 4
+    scratch += [dma((members, CHUNKS))] * 2
+    scratch += [dma((members,))] * 2
+    scratch += [dma((spaces,))] * 2
+    scratch += [dma((members,))] * 6
+    scratch += [dma((spaces,))] * 8
+    scratch += [dma((members,))] * 4
+    whole = pl.BlockSpec(memory_space=pltpu.VMEM)
+    pred, loss, gout, gmsg = pl.pallas_call(
+        functools.partial(step_kernel, spaces, members),
+        out_shape=(
+            jax.ShapeDtypeStruct((1, varn, grid), BF16),
+            jax.ShapeDtypeStruct((1,), F32),
+            jax.ShapeDtypeStruct((latent, varn), F32),
+            jax.ShapeDtypeStruct((latent, latent), BF16),
+        ),
+        in_specs=[whole] * 16,
+        out_specs=(whole, pl.BlockSpec(memory_space=pltpu.SMEM), whole, whole),
+        scratch_shapes=scratch,
+        compiler_params=pltpu.CompilerParams(
+            collective_id=0, has_side_effects=True, vmem_limit_bytes=50 * 1024 * 1024
+        ),
+    )(
+        starting_states, observed, mesh_feat, enc_send, enc_edges, dec_send, dec_edges,
+        dec_edges.T, w_in, w_src, w_dst, w_enc, w_msg, w_self, w_hid, decoder_variable_matrix.T,
+    )
+    return pred, loss, gout, gmsg
+
+
+def fits(spaces, members, latent, ecap, dcap):
+    return (
+        latent % (128 * members) == 0
+        and latent // members == 128
+        and ecap % 128 == 0
+        and dcap % 16 == 0
+        and latent % (16 * spaces) == 0
+        and 128 % (8 * spaces) == 0
+    )
+
+
+def chosen(*args):
+    spaces, members = lax.axis_size("space"), lax.axis_size("mem")
+    if fits(spaces, members, args[8].shape[0], args[3].shape[2], args[5].shape[2]):
+        return fused(*args)
+    return local(*args)
 
 
 def silu_slope(argument):
@@ -170,4 +605,5 @@
         P(),
     )
     out_specs = (P(("grp", "mem"), None, "space"), P("grp"), P("grp", None), P("grp", None))
-    return jax.shard_map(local, mesh=mesh, in_specs=in_specs, out_specs=out_specs, check_vma=False)
+    return jax.shard_map(
+        chosen, mesh=mesh, in_specs=in_specs, out_specs=out_specs, check_vma=False)

time: 265 us -> 72 us (0.27)
  blocking collectives: 88.8 us -> 0 us
  local copies, waits for them, and re-layouts: 77.7 us -> 10.8 us
  Pallas kernels: 0 us -> 57.5 us
  other arithmetic: 46.9 us -> 0 us
  matrix products: 15.4 us -> 0 us
  between operations: 17.4 us -> 2.48 us
  starting transfers between devices: 11.4 us -> 0 us
  waiting for transfers between devices: 5.95 us -> 0 us
    psum x2 -> x0, blocking collectives: 79.7 us -> none  [the longest x1 69.9 us: local(): grad_out, grad_msg = lax.psum((part_out, part_msg), ('space', 'mem'))]
    pallas_call x0 -> x1, Pallas kernels: none -> 57.5 us  [fused(): pl.pallas_call(functools.partial(step_kernel, spaces, members), out_shape...]
    gather x5 -> x0, local copies, waits for them, and re-layouts: 34.3 us -> none  [the longest x2 22.3 us: local(): jnp.take(message, dec_edges, axis=0).astype(jnp.float32)]
    scatter-add x1 -> x0, other arithmetic: 23.8 us -> none  [local(): jax.ops.segment_sum(edge_grad.reshape(-1, edge_grad.shape[2]), dec_edges....]
    add x2 -> x0, local copies, waits for them, and re-layouts: 15.4 us -> none  [local(): jnp.take(message, dec_edges, axis=0).astype(jnp.float32)]
    mul x2 -> x0, local copies, waits for them, and re-layouts: 15.4 us -> none  [local(): updated_grad[:, None, :] * silu_slope(decoder_in) / dec_edges.shape[1]]
    dot_general x11 -> x0, matrix products: 15.4 us -> none  [the longest x1 3.06 us: local(): jnp.einsum('gk,hk->gh', pre_grad, w_hid, preferred_element_type=jnp.float32)]
    reduce_sum x10 -> x0, other arithmetic: 12.3 us -> none  [the longest x1 4.85 us: local(): jnp.mean(jax.nn.silu(decoder_in), axis=1)]
  transfers between devices with their start and end apart: 3 -> 0, of which waited for: 1 -> 0; matrix products, arithmetic and copies ran while one was open for 24% -> 0% of each run, Pallas kernels for 0% -> 0%
where the time goes in v1:
time: 72 us; the launch traced here: 70.7 us
  Pallas kernels  57.5 us (80%)
  local copies, waits for them, and re-layouts  10.8 us (15%)
  between operations  2.48 us (3%)
    pallas_call x1, Pallas kernels, fused(): pl.pallas_call(functools.partial(step_kernel, spaces, members), out_shape...  57.5 us
    unnamed x26, local copies, waits for them, and re-layouts  9.96 us

profile of v1, /device:TPU:0, one launch (start us, length us, event | category | flops | bytes accessed | tf_op | source)
XLA Modules:
  0.0 70.7 jit_solution(2897582680465313548)
XLA Ops:
  0.6 0.0 copy-start
  0.6 0.9 %copy.19.eedge_ref = s32[128,16]{1,0:T(8,128)S(1)} copy(s32[128,16]{0,1:T(8,128)} %param.19) | data formatting | bytes 16384 | tf_op args[4]
  1.5 0.0 copy-start.8
  1.5 0.0 copy-start.9
  1.5 0.0 copy-start.10
  1.5 1.0 %copy.20.dedge_ref = s32[1024,3]{1,0:T(8,128)S(1)} copy(s32[1024,3]{0,1:T(4,128)} %param.21) | data formatting | bytes 24576 | tf_op args[6]
  2.5 0.0 copy-done
  2.5 0.0 copy-done.8
  2.5 0.0 copy-done.9
  2.5 0.0 copy-done.10
  2.5 0.0 copy-start.1
  2.6 1.0 %copy-done.1 = bf16[512,512]{1,0:T(8,128)(2,1)S(1)} copy-done((bf16[512,512]{1,0:T(8,128)(2,1)S(1)}, bf16[512,512]{1,0:T(8,128)(2,1)}, u32[]{:S(2)}) %copy-start.1) | copy-done | bytes 524312
  3.6 0.0 copy-start.2
  3.6 1.0 %copy-done.2 = bf16[512,512]{1,0:T(8,128)(2,1)S(1)} copy-done((bf16[512,512]{1,0:T(8,128)(2,1)S(1)}, bf16[512,512]{1,0:T(8,128)(2,1)}, u32[]{:S(2)}) %copy-start.2) | copy-done | bytes 524312
  4.6 0.0 copy-start.3
  4.6 0.9 %copy-done.3 = bf16[1,100,1024]{2,1,0:T(8,128)(2,1)S(1)} copy-done((bf16[1,100,1024]{2,1,0:T(8,128)(2,1)S(1)}, bf16[1,100,1024]{2,1,0:T(8,128)(2,1)}, u32[]{:S(2)}) %copy-start.3) | copy-done | bytes 204824
  5.6 0.0 copy-start.4
  5.6 0.9 %copy-done.4 = bf16[100,1024]{1,0:T(8,128)(2,1)S(1)} copy-done((bf16[100,1024]{1,0:T(8,128)(2,1)S(1)}, bf16[100,1024]{1,0:T(8,128)(2,1)}, u32[]{:S(2)}) %copy-start.4) | copy-done | bytes 204824
  6.5 0.0 copy-start.5
  6.5 0.9 %copy-done.5 = bf16[128,512]{1,0:T(8,128)(2,1)S(1)} copy-done((bf16[128,512]{1,0:T(8,128)(2,1)S(1)}, bf16[128,512]{1,0:T(8,128)(2,1)}, u32[]{:S(2)}) %copy-start.5) | copy-done | bytes 131096
  7.4 0.0 copy-start.6
  7.4 0.9 %copy-done.6 = bf16[100,512]{1,0:T(8,128)(2,1)S(1)} copy-done((bf16[100,512]{1,0:T(8,128)(2,1)S(1)}, bf16[100,512]{1,0:T(8,128)(2,1)}, u32[]{:S(2)}) %copy-start.6) | copy-done | bytes 102424
  8.3 0.0 copy-start.7
  8.3 0.9 %copy-done.7 = bf16[512,100]{0,1:T(8,128)(2,1)S(1)} copy-done((bf16[512,100]{0,1:T(8,128)(2,1)S(1)}, bf16[512,100]{0,1:T(8,128)(2,1)}, u32[]{:S(2)}) %copy-start.7) | copy-done | bytes 102424
  9.2 57.5 %shard_map.174 = (bf16[1,100,1024]{2,1,0:T(8,128)(2,1)S(1)}, f32[1]{0:T(128)}, f32[512,100]{1,0:T(8,128)S(1)}, bf16[512,512]{1,0:T(8,128)(2,1)S(1)}) custom-call(bf16[1,100,1024]{2,1,0:T(8,128)(2,1)S(1)} %copy-done.3, bf16[100,1024]{1,0:T(8,128)(2,1)S(1)} %copy-done.4, bf16[128,512]{1,0:T(8,128)(2,1)S(1)} %copy-done.5, s32[1,4,128]{2,1,0:T(4,128)S(1)} %copy-done.9, ...), custom_call_target="tpu_custom_call" | custom-call | tf_op jit(solution)/shard_map/pallas_call | solution.py:405
  66.7 0.8 %copy.21 = f32[512,100]{0,1:T(8,128)} copy(f32[512,100]{1,0:T(8,128)S(1)} %get-tuple-element.6) | data formatting | bytes 409600 | tf_op jit(solution)/shard_map/pallas_call | solution.py:405
  67.5 0.7 copy.25
  68.8 0.8 %copy.27 = bf16[512,512]{1,0:T(8,128)(2,1)} copy(bf16[512,512]{1,0:T(8,128)(2,1)S(1)} %get-tuple-element.15) | data formatting | bytes 1048576
Async XLA Ops:
  0.6 1.9 %copy-start = (bf16[512,512]{1,0:T(8,128)(2,1)S(1)}, bf16[512,512]{1,0:T(8,128)(2,1)}, u32[]{:S(2)}) copy-start(bf16[512,512]{1,0:T(8,128)(2,1)} %w_src_ref.1) | copy-start | bytes 1572868
  1.5 1.0 %copy-start.8 = (s32[1024,3]{0,1:T(4,128)S(1)}, s32[1024,3]{0,1:T(4,128)}, u32[]{:S(2)}) copy-start(s32[1024,3]{0,1:T(4,128)} %param.21) | copy-start | bytes 36868
  1.5 1.0 %copy-start.9 = (s32[1,4,128]{2,1,0:T(4,128)S(1)}, s32[1,4,128]{2,1,0:T(4,128)}, u32[]{:S(2)}) copy-start(s32[1,4,128]{2,1,0:T(4,128)} %esend_ref.1) | copy-start | bytes 6148
  1.5 1.0 %copy-start.10 = (s32[1,4,32]{2,1,0:T(4,128)S(1)}, s32[1,4,32]{2,1,0:T(4,128)}, u32[]{:S(2)}) copy-start(s32[1,4,32]{2,1,0:T(4,128)} %dsend_ref.1) | copy-start | bytes 1540
  2.5 1.0 %copy-start.1 = (bf16[512,512]{1,0:T(8,128)(2,1)S(1)}, bf16[512,512]{1,0:T(8,128)(2,1)}, u32[]{:S(2)}) copy-start(bf16[512,512]{1,0:T(8,128)(2,1)} %w_dst_ref.1) | copy-start | bytes 1572868
  3.6 1.0 %copy-start.2 = (bf16[512,512]{1,0:T(8,128)(2,1)S(1)}, bf16[512,512]{1,0:T(8,128)(2,1)}, u32[]{:S(2)}) copy-start(bf16[512,512]{1,0:T(8,128)(2,1)} %w_enc_ref.1) | copy-start | bytes 1572868
  4.6 0.9 %copy-start.3 = (bf16[1,100,1024]{2,1,0:T(8,128)(2,1)S(1)}, bf16[1,100,1024]{2,1,0:T(8,128)(2,1)}, u32[]{:S(2)}) copy-start(bf16[1,100,1024]{2,1,0:T(8,128)(2,1)} %x_ref.1) | copy-start | bytes 614404
  5.6 0.9 %copy-start.4 = (bf16[100,1024]{1,0:T(8,128)(2,1)S(1)}, bf16[100,1024]{1,0:T(8,128)(2,1)}, u32[]{:S(2)}) copy-start(bf16[100,1024]{1,0:T(8,128)(2,1)} %obs_ref.1) | copy-start | bytes 614404
  6.5 0.9 %copy-start.5 = (bf16[128,512]{1,0:T(8,128)(2,1)S(1)}, bf16[128,512]{1,0:T(8,128)(2,1)}, u32[]{:S(2)}) copy-start(bf16[128,512]{1,0:T(8,128)(2,1)} %feat_ref.1) | copy-start | bytes 393220
  7.4 0.9 %copy-start.6 = (bf16[100,512]{1,0:T(8,128)(2,1)S(1)}, bf16[100,512]{1,0:T(8,128)(2,1)}, u32[]{:S(2)}) copy-start(bf16[100,512]{1,0:T(8,128)(2,1)} %w_in_ref.1) | copy-start | bytes 307204
  8.3 0.9 %copy-start.7 = (bf16[512,100]{0,1:T(8,128)(2,1)S(1)}, bf16[512,100]{0,1:T(8,128)(2,1)}, u32[]{:S(2)}) copy-start(bf16[512,100]{0,1:T(8,128)(2,1)} %param.29) | copy-start | bytes 307204

commit v2 on v1

--- a/solution.py
+++ b/solution.py
@@ -9,6 +9,8 @@
 from jax.sharding import PartitionSpec as P
 
 MESH = pl.DeviceIdType.MESH
+HBM = pltpu.HBM
+ANY = pl.BlockSpec(memory_space=pl.ANY)
 F32 = jnp.float32
 BF16 = jnp.bfloat16
 ROWS = 112
@@ -40,102 +42,116 @@
 
 def step_kernel(
     spaces, members,
-    x_ref, obs_ref, feat_ref, esend_ref, eedge_ref, dsend_ref, dedge_ref, dedge_t_ref,
+    x_hbm, obs_hbm, feat_hbm, esend_hbm, eedge_hbm, dsend_hbm, dedge_hbm,
+    w_in_hbm, w_src_hbm, w_dst_hbm, w_enc_hbm, w_msg_hbm, w_self_hbm, w_hid_hbm, dvm_t_hbm,
+    pred_ref, loss_ref, gout_ref, gmsg_ref,
+    x_ref, obs_ref, feat_ref, esend_ref, eedge_ref, dsend_ref, dedge_ref,
     w_in_ref, w_src_ref, w_dst_ref, w_enc_ref, w_msg_ref, w_self_ref, w_hid_ref, dvm_t_ref,
-    pred_ref, loss_ref, gout_ref, gmsg_ref,
-    xp, obsp, winp, dvmp,
-    xs_send, xs_recv, gl, self_term, ehot, dhot, dhot_t, arr_gl, arr, nq,
+    xp, obsp, winp, dvmp, dedges,
+    xs_send, xs_recv, gl, self_term, ehot, dhot, dhot_t, arr, nq,
     ms_send, ma, dec_in, hid, act, ens, st, st_recv, loss_s, loss_r, fgs,
-    gos, gor, gs, gq, aall, at, q32, qb, q_recv, gq32, gq_recv, fin, gfin,
-    x_ss, x_rs, m_ss, m_rs, e_ss, e_rs, a_ss, a_rs, s_ss, s_rs, l_ss, l_rs,
-    o_ss, o_rs, g_ss, g_rs, zq_ss, zq_rs, zo_ss, zo_rs, c1_ss, c1_rs, d1_ss, d1_rs,
-    c2_ss, c2_rs, d2_ss, d2_rs,
+    gos, gor, gs, gq, aall, at, q32, qb, q_recv, fin,
+    in_sem, x_ss, x_rs, m_ss, m_rs, s_ss, s_rs, zq_ss, zq_rs, c1_ss, c1_rs,
+    l_ss, l_rs, o_ss, o_rs, g_ss, g_rs, a_ss, a_rs, e_ss, e_rs, c2_ss, c2_rs,
 ):
     grp, sp, me = lax.axis_index("grp"), lax.axis_index("space"), lax.axis_index("mem")
+    partner = [me, me + 1 - 2 * lax.rem(me, 2), lax.rem(me + 2, 4), 3 - me]
     varn, grid = obs_ref.shape
     latent = w_src_ref.shape[0]
     nodes = feat_ref.shape[0]
     ecap, dcap = esend_ref.shape[2], dsend_ref.shape[2]
     slots, dslots = spaces * ecap, spaces * dcap
-    k_enc, k_dec = eedge_ref.shape[1], dedge_ref.shape[1]
+    k_enc, k_dec = eedge_ref.shape[0], dedge_ref.shape[0]
     part = grid // CHUNKS
     entries = varn * grid * spaces
     quarter = latent // members
     zrows = latent // spaces
+    orows = 128 // spaces
+
+    loads = {}
+    order = (
+        (x_hbm, x_ref), (esend_hbm, esend_ref), (w_in_hbm, w_in_ref), (feat_hbm, feat_ref),
+        (w_dst_hbm, w_dst_ref), (eedge_hbm, eedge_ref), (w_src_hbm, w_src_ref),
+        (w_enc_hbm, w_enc_ref), (dsend_hbm, dsend_ref), (dedge_hbm, dedge_ref),
+        (w_self_hbm, w_self_ref), (w_msg_hbm, w_msg_ref), (w_hid_hbm, w_hid_ref),
+        (dvm_t_hbm, dvm_t_ref), (obs_hbm, obs_ref),
+    )
+    for i, (far, near) in enumerate(order):
+        loads[id(near)] = pltpu.make_async_copy(far, near, in_sem.at[i])
+        loads[id(near)].start()
+
+    def ready(*refs):
+        for ref in refs:
+            loads.pop(id(ref)).wait()
 
     def space_at(o):
         return lax.rem(sp + o, spaces)
 
-    def mem_at(o):
-        return lax.rem(me + o, members)
-
     def to_space(src, dst, ss, rs, o):
-        return pltpu.make_async_remote_copy(
+        copy = pltpu.make_async_remote_copy(
             src_ref=src, dst_ref=dst, send_sem=ss.at[o], recv_sem=rs.at[o],
             device_id=(grp, space_at(o), me), device_id_type=MESH,
         )
-
-    def to_mem(src, dst, ss, rs, o):
-        return pltpu.make_async_remote_copy(
+        copy.start()
+        return copy
+
+    def to_mem(src, dst, ss, rs, j):
+        copy = pltpu.make_async_remote_copy(
             src_ref=src, dst_ref=dst, send_sem=ss, recv_sem=rs,
-            device_id=(grp, sp, mem_at(o)), device_id_type=MESH,
+            device_id=(grp, sp, partner[j]), device_id_type=MESH,
         )
+        copy.start()
+        return copy
 
     barrier = pltpu.get_barrier_semaphore()
     for o in range(1, spaces):
         pl.semaphore_signal(barrier, inc=1, device_id=(grp, space_at(o), me), device_id_type=MESH)
-    for o in range(1, members):
-        pl.semaphore_signal(barrier, inc=1, device_id=(grp, sp, mem_at(o)), device_id_type=MESH)
-
+    for j in range(1, members):
+        pl.semaphore_signal(barrier, inc=1, device_id=(grp, sp, partner[j]), device_id_type=MESH)
+
+    ready(x_ref, esend_ref)
     xp[96:ROWS, :] = jnp.zeros((ROWS - 96, grid), BF16)
     xp[0:varn, :] = x_ref[0]
-    winp[96:ROWS, :] = jnp.zeros((ROWS - 96, latent), BF16)
-    winp[0:varn, :] = w_in_ref[...]
-
     grid_rows = lax.broadcasted_iota(jnp.int32, (grid, ecap), 0)
-    xs = []
-    waited = False
+    xs = {}
     for o in list(range(1, spaces)) + [0]:
         row = esend_ref[0, pl.ds(space_at(o), 1), :]
-        hot = one_hot(grid_rows == row)
-        picked = dot(xp[...], hot).astype(BF16)
+        picked = dot(xp[...], one_hot(grid_rows == row)).astype(BF16)
         if o == 0:
             xs_recv[sp] = picked
         else:
             xs_send[o] = picked
-            if not waited:
+            if not xs:
                 pl.semaphore_wait(barrier, spaces + members - 2)
-                waited = True
-            copy = to_space(xs_send.at[o], xs_recv.at[sp], x_ss, x_rs, o)
-            copy.start()
-            xs.append(copy)
-
-    obsp[96:ROWS, :] = jnp.zeros((ROWS - 96, grid), BF16)
-    obsp[0:varn, :] = obs_ref[...]
-    dvmp[96:ROWS, :] = jnp.zeros((ROWS - 96, latent), BF16)
-    dvmp[0:varn, :] = dvm_t_ref[...]
+            xs[o] = to_space(xs_send.at[o], xs_recv.at[sp], x_ss, x_rs, o)
+
+    ready(w_in_ref, feat_ref, w_dst_ref, eedge_ref)
+    winp[96:ROWS, :] = jnp.zeros((ROWS - 96, latent), BF16)
+    winp[0:varn, :] = w_in_ref[...]
     nq[...] = dot(feat_ref[...], w_dst_ref[...]).astype(BF16).astype(F32)
     slot_cols = lax.broadcasted_iota(jnp.int32, (nodes, slots), 1)
+    columns = eedge_ref[...].T
     for k in range(k_enc):
-        ehot[k * nodes:(k + 1) * nodes, :] = one_hot(slot_cols == eedge_ref[:, k:k + 1])
-    for c in range(CHUNKS):
-        rows = slice(c * part, (c + 1) * part)
-        gl[rows, :] = silu(dot(xp[:, rows], winp[...], (0, 0))).astype(BF16)
-
-    for copy in xs:
-        copy.wait()
-    for s in range(spaces):
-        arr_gl[s * ecap:(s + 1) * ecap, :] = silu(dot(xs_recv[s], winp[...], (0, 0))).astype(BF16)
-    arr[...] = dot(arr_gl[...], w_src_ref[...]).astype(BF16)
+        ehot[k * nodes:(k + 1) * nodes, :] = one_hot(slot_cols == columns[:, k:k + 1])
+
+    ready(w_src_ref, w_enc_ref)
+    for o in range(spaces):
+        if o:
+            xs[o].wait()
+        source = lax.rem(sp + spaces - o, spaces)
+        embedded = silu(dot(xs_recv[source], winp[...], (0, 0))).astype(BF16)
+        arr[source] = dot(embedded, w_src_ref[...]).astype(BF16)
+    arrived = arr[...].reshape(slots, latent)
     total = jnp.zeros((nodes, latent), F32)
     group = 4
     for k in range(0, k_enc, group):
-        v = dot(ehot[k * nodes:(k + group) * nodes, :], arr[...])
+        v = dot(ehot[k * nodes:(k + group) * nodes, :], arrived)
         for i in range(group):
             total += silu(v[i * nodes:(i + 1) * nodes, :] + nq[...])
     aggregate = (total * (1.0 / k_enc)).astype(BF16)
     mesh_latent = (feat_ref[...].astype(F32) + dot(aggregate, w_enc_ref[...])).astype(BF16)
 
+    ready(dsend_ref)
     node_rows = lax.broadcasted_iota(jnp.int32, (nodes, dcap), 0)
     ms = []
     for o in list(range(1, spaces)) + [0]:
@@ -145,24 +161,33 @@
             ma[sp] = picked
         else:
             ms_send[o] = picked
-            copy = to_space(ms_send.at[o], ma.at[sp], m_ss, m_rs, o)
-            copy.start()
-            ms.append(copy)
-    dcols = lax.broadcasted_iota(jnp.int32, (grid, dslots), 1)
-    drows = lax.broadcasted_iota(jnp.int32, (dslots, grid), 0)
-    for k in range(k_dec):
-        dhot[k] = one_hot(dcols == dedge_ref[:, k:k + 1])
-        dhot_t[k] = one_hot(drows == dedge_t_ref[k:k + 1, :])
+            ms.append(to_space(ms_send.at[o], ma.at[sp], m_ss, m_rs, o))
+    ready(dedge_ref, w_self_ref, w_msg_ref, w_hid_ref, dvm_t_ref, obs_ref)
     for c in range(CHUNKS):
         rows = slice(c * part, (c + 1) * part)
-        self_term[rows, :] = dot(gl[rows, :], w_self_ref[...])
+        latents = silu(dot(xp[:, rows], winp[...], (0, 0))).astype(BF16)
+        gl[rows, :] = latents
+        self_term[rows, :] = dot(latents, w_self_ref[...])
+    dvmp[96:ROWS, :] = jnp.zeros((ROWS - 96, latent), BF16)
+    dvmp[0:varn, :] = dvm_t_ref[...]
+    dedges[...] = jnp.zeros((8, grid), jnp.int32)
+    dedges[0:k_dec, :] = dedge_ref[...]
+    dcolumns = dedges[...].T
+    dcols = lax.broadcasted_iota(jnp.int32, (grid, dslots), 1)
+    for k in range(k_dec):
+        dhot[k] = one_hot(dcols == dcolumns[:, k:k + 1])
     for copy in ms:
         copy.wait()
 
     arrivals = ma[...].reshape(dslots, latent)
     aall[0] = arrivals
     message = dot(arrivals, w_msg_ref[...]).astype(BF16)
-    es = []
+    near, far, passed = [], [], []
+
+    def pass_on(c):
+        far[c].wait()
+        passed.append(to_mem(ens.at[2, c], ens.at[3, c], e_ss.at[3, c], e_rs.at[3, c], 1))
+
     for c in range(CHUNKS):
         rows = slice(c * part, (c + 1) * part)
         acc = jnp.zeros((part, latent), F32)
@@ -179,24 +204,23 @@
         increment = dot(dvmp[...], response, (1, 1))
         predicted = (xp[:, rows].astype(F32) + increment).astype(BF16)
         ens[0, c] = predicted
+        far.append(to_mem(ens.at[0, c], ens.at[2, c], e_ss.at[2, c], e_rs.at[2, c], 2))
+        near.append(to_mem(ens.at[0, c], ens.at[1, c], e_ss.at[1, c], e_rs.at[1, c], 1))
         pred_ref[0, :, rows] = predicted[0:varn, :]
-        for o in range(1, members):
-            copy = to_mem(
-                ens.at[0, c], ens.at[members - o, c], e_ss.at[o, c], e_rs.at[o, c], o
-            )
-            copy.start()
-            es.append(copy)
-    as_ = []
-    for o in range(1, members):
-        copy = to_mem(aall.at[0], aall.at[members - o], a_ss.at[o], a_rs.at[o], o)
-        copy.start()
-        as_.append(copy)
-
+        if c:
+            pass_on(c - 1)
+    a_far = to_mem(aall.at[0], aall.at[2], a_ss.at[2], a_rs.at[2], 2)
+    a_near = to_mem(aall.at[0], aall.at[1], a_ss.at[1], a_rs.at[1], 1)
+
+    obsp[96:ROWS, :] = jnp.zeros((ROWS - 96, grid), BF16)
+    obsp[0:varn, :] = obs_ref[...]
     for c in range(CHUNKS):
         rows = slice(c * part, (c + 1) * part)
         hid[rows, :] = slope(hid[rows, :])
         for k in range(k_dec):
             dec_in[k, rows, :] = slope(dec_in[k, rows, :]) * (1.0 / k_dec)
+        if c == 1:
+            pass_on(CHUNKS - 1)
 
     def folded(d):
         d = (d * d).reshape(ROWS // 8, 8, part).sum(axis=0)
@@ -206,21 +230,23 @@
         return out
 
     sums = [jnp.zeros((8, 128), F32) for _ in range(members)]
-    for copy in es:
-        copy.wait()
     for c in range(CHUNKS):
         rows = slice(c * part, (c + 1) * part)
+        near[c].wait()
         mine = ens[0, c].astype(F32)
         sums[0] += folded(mine - obsp[:, rows].astype(F32))
-        for j in range(1, members):
-            sums[j] += folded(mine - ens[j, c].astype(F32))
+        sums[1] += folded(mine - ens[1, c].astype(F32))
+        sums[2] += folded(mine - ens[2, c].astype(F32))
+        passed[c].wait()
+        sums[3] += folded(mine - ens[3, c].astype(F32))
     for j in range(members):
         st[j] = sums[j]
-    ss = []
-    for o in range(1, spaces):
-        copy = to_space(st, st_recv.at[o], s_ss, s_rs, o)
-        copy.start()
-        ss.append(copy)
+    ss = [to_space(st, st_recv.at[o], s_ss, s_rs, o) for o in range(1, spaces)]
+    drows = lax.broadcasted_iota(jnp.int32, (dslots, grid), 0)
+    for k in range(k_dec):
+        dhot_t[k] = one_hot(drows == dedges[k:k + 1, :])
+    a_far.wait()
+    a_passed = to_mem(aall.at[2], aall.at[3], a_ss.at[3], a_rs.at[3], 1)
     for copy in ss:
         copy.wait()
     tot = st[...]
@@ -232,11 +258,6 @@
     for j in range(1, members):
         my_loss -= root[j] / (2.0 * members * members)
     loss_s[...] = jnp.broadcast_to(my_loss, (8, 128))
-    ls = []
-    for o in range(1, members):
-        copy = to_mem(loss_s, loss_r.at[o], l_ss.at[o], l_rs.at[o], o)
-        copy.start()
-        ls.append(copy)
     scale = members * math.sqrt(entries)
     first = scale / (members * entries * error)
     pulls = [scale / (members * members * entries * root[j]) for j in range(1, members)]
@@ -252,13 +273,12 @@
         fgs[c] = fg
         gout += dot(fg, act[rows, :])
     for m in range(members):
-        gos[m, 0:ROWS, :] = gout[:, m * quarter:(m + 1) * quarter]
-        gos[m, ROWS:128, :] = jnp.zeros((128 - ROWS, quarter), F32)
-    os_ = []
-    for o in range(1, members):
-        copy = to_mem(gos.at[mem_at(o)], gor.at[o], o_ss.at[o], o_rs.at[o], o)
-        copy.start()
-        os_.append(copy)
+        gos[m, 0:ROWS, :] = gout[:, m * quarter:(m + 1) * quarter].astype(BF16)
+        gos[m, ROWS:128, :] = jnp.zeros((128 - ROWS, quarter), BF16)
+    os_, ls = [], []
+    for j in range(1, members):
+        os_.append(to_mem(gos.at[partner[j]], gor.at[j], o_ss.at[j], o_rs.at[j], j))
+        ls.append(to_mem(loss_s, loss_r.at[j], l_ss.at[j], l_rs.at[j], j))
 
     mgrad = jnp.zeros((dslots, latent), F32)
     for c in range(CHUNKS):
@@ -272,87 +292,82 @@
     for m in range(members):
         gs[m] = mgrad[:, m * quarter:(m + 1) * quarter].astype(BF16)
     gsent = []
-    for o in range(1, members):
-        copy = to_mem(gs.at[mem_at(o)], gq.at[members - o], g_ss.at[o], g_rs.at[o], o)
-        copy.start()
-        gsent.append(copy)
+    for j in (2, 3, 1):
+        gsent.append(to_mem(gs.at[partner[j]], gq.at[j], g_ss.at[j], g_rs.at[j], j))
     gq[0] = gs[me]
-    for copy in as_:
-        copy.wait()
+    a_near.wait()
+    a_passed.wait()
     for j in range(members):
         at[:, j * dslots:(j + 1) * dslots] = aall[j].astype(F32).T.astype(BF16)
     for copy in os_:
         copy.wait()
-    oq = gos[me]
-    for o in range(1, members):
-        oq += gor[o]
-    gq32[...] = oq.reshape(spaces, 128 // spaces, quarter)
-    zo = []
-    for o in range(1, spaces):
-        copy = to_space(gq32.at[space_at(o)], gq_recv.at[o], zo_ss, zo_rs, o)
-        copy.start()
-        zo.append(copy)
+    oq = gos[me].astype(F32)
+    for j in range(1, members):
+        oq += gor[j].astype(F32)
+    oq = oq.reshape(spaces, orows, quarter)
+    q32[:, zrows:, :] = oq
+    qb[:, zrows:, :] = oq.astype(BF16)
     for copy in gsent:
         copy.wait()
     q = dot(at[...], gq[...].reshape(members * dslots, quarter)).reshape(spaces, zrows, quarter)
-    q32[...] = q
-    qb[...] = q.astype(BF16)
-    zq = []
-    for o in range(1, spaces):
-        copy = to_space(qb.at[space_at(o)], q_recv.at[o], zq_ss, zq_rs, o)
-        copy.start()
-        zq.append(copy)
-    for copy in zo:
-        copy.wait()
-    gsum = gq32[sp]
-    for o in range(1, spaces):
-        gsum += gq_recv[o]
-    gfin[me, sp] = gsum
-    d1 = []
-    for o in range(1, spaces):
-        copy = to_space(gfin.at[me, sp], gfin.at[me, sp], d1_ss, d1_rs, o)
-        copy.start()
-        d1.append(copy)
-    for copy in zq:
-        copy.wait()
+    q32[:, 0:zrows, :] = q
+    qb[:, 0:zrows, :] = q.astype(BF16)
+    zq = [
+        to_space(qb.at[space_at(o)], q_recv.at[o], zq_ss, zq_rs, o) for o in range(1, spaces)
+    ]
     r = q32[sp]
     for o in range(1, spaces):
+        zq[o - 1].wait()
         r += q_recv[o].astype(F32)
-    fin[me, sp] = r.astype(BF16)
-    c1 = []
-    for o in range(1, spaces):
-        copy = to_space(fin.at[me, sp], fin.at[me, sp], c1_ss, c1_rs, o)
-        copy.start()
-        c1.append(copy)
-    for copy in d1:
-        copy.wait()
-    d2 = []
-    for o in range(1, members):
-        copy = to_mem(gfin.at[me], gfin.at[me], d2_ss.at[o], d2_rs.at[o], o)
-        copy.start()
-        d2.append(copy)
-    for copy in c1:
-        copy.wait()
-    c2 = []
-    for o in range(1, members):
-        copy = to_mem(fin.at[me], fin.at[me], c2_ss.at[o], c2_rs.at[o], o)
-        copy.start()
-        c2.append(copy)
+    fin[0, sp] = r.astype(BF16)
+
+    c1 = [
+        to_space(fin.at[0, sp], fin.at[0, sp], c1_ss, c1_rs, o) for o in range(1, spaces)
+    ]
+    c_far, c_near, c_passed = [], [], []
+    for o in range(spaces):
+        if o:
+            c1[o - 1].wait()
+        at_ = lax.rem(sp + spaces - o, spaces)
+        c_far.append(to_mem(fin.at[0, at_], fin.at[2, at_], c2_ss.at[2, o], c2_rs.at[2, o], 2))
+        c_near.append(to_mem(fin.at[0, at_], fin.at[1, at_], c2_ss.at[1, o], c2_rs.at[1, o], 1))
+    for o in range(spaces):
+        at_ = lax.rem(sp + spaces - o, spaces)
+        c_far[o].wait()
+        c_passed.append(to_mem(fin.at[2, at_], fin.at[3, at_], c2_ss.at[3, o], c2_rs.at[3, o], 1))
     for copy in ls:
         copy.wait()
     all_loss = loss_s[...]
-    for o in range(1, members):
-        all_loss += loss_r[o]
+    for j in range(1, members):
+        all_loss += loss_r[j]
     loss_ref[0] = jnp.max(all_loss)
-    for copy in d2:
+    for copy in c_near + c_passed:
         copy.wait()
     for m in range(members):
-        block = gfin[m].reshape(128, quarter).T
-        gout_ref[m * quarter:(m + 1) * quarter, :] = block[:, 0:varn]
-    for copy in c2:
+        if m == 0:
+            slot = me
+        elif m == 1:
+            slot = partner[1]
+        elif m == 2:
+            slot = partner[2]
+        else:
+            slot = partner[3]
+        cols = slice(m * quarter, (m + 1) * quarter)
+        block = fin[slot]
+        gmsg_ref[:, cols] = block[:, 0:zrows, :].reshape(latent, quarter)
+        gout_ref[:, cols] = block[:, zrows:, :].reshape(128, quarter)[0:varn, :].astype(F32)
+
+
+def copy_kernel(a, b, c, d, a_out, b_out, c_out, d_out, sem):
+    copies = [
+        pltpu.make_async_copy(x, y, sem.at[i])
+        for i, (x, y) in enumerate(((a, a_out), (c, c_out), (d, d_out)))
+    ]
+    for copy in copies:
+        copy.start()
+    b_out[0] = b[0]
+    for copy in copies:
         copy.wait()
-    for m in range(members):
-        gmsg_ref[:, m * quarter:(m + 1) * quarter] = fin[m].reshape(latent, quarter)
 
 
 def fused(
@@ -368,64 +383,72 @@
     k_enc, k_dec = enc_edges.shape[1], dec_edges.shape[1]
     part = grid // CHUNKS
     quarter = latent // members
-    zrows = latent // spaces
+    zrows = latent // spaces + 128 // spaces
     vmem = pltpu.VMEM
-    scratch = [
+    operands = (
+        starting_states, observed, mesh_feat, enc_send, enc_edges.T, dec_send, dec_edges.T,
+        w_in, w_src, w_dst, w_enc, w_msg, w_self, w_hid, decoder_variable_matrix.T,
+    )
+    scratch = [vmem(operand.shape, operand.dtype) for operand in operands]
+    scratch += [
         vmem((ROWS, grid), BF16), vmem((ROWS, grid), BF16),
-        vmem((ROWS, latent), BF16), vmem((ROWS, latent), BF16),
+        vmem((ROWS, latent), BF16), vmem((ROWS, latent), BF16), vmem((8, grid), jnp.int32),
         vmem((spaces, ROWS, ecap), BF16), vmem((spaces, ROWS, ecap), BF16),
         vmem((grid, latent), BF16), vmem((grid, latent), F32),
         vmem((k_enc * nodes, slots), BF16),
         vmem((k_dec, grid, dslots), BF16), vmem((k_dec, dslots, grid), BF16),
-        vmem((slots, latent), BF16), vmem((slots, latent), BF16), vmem((nodes, latent), F32),
+        vmem((spaces, ecap, latent), BF16), vmem((nodes, latent), F32),
         vmem((spaces, dcap, latent), BF16), vmem((spaces, dcap, latent), BF16),
         vmem((k_dec, grid, latent), F32), vmem((grid, latent), F32), vmem((grid, latent), BF16),
         vmem((members, CHUNKS, ROWS, part), BF16),
         vmem((members, 8, 128), F32), vmem((spaces, members, 8, 128), F32),
         vmem((8, 128), F32), vmem((members, 8, 128), F32),
         vmem((CHUNKS, ROWS, part), BF16),
-        vmem((members, 128, quarter), F32), vmem((members, 128, quarter), F32),
+        vmem((members, 128, quarter), BF16), vmem((members, 128, quarter), BF16),
         vmem((members, dslots, quarter), BF16), vmem((members, dslots, quarter), BF16),
         vmem((members, dslots, latent), BF16), vmem((latent, members * dslots), BF16),
         vmem((spaces, zrows, quarter), F32), vmem((spaces, zrows, quarter), BF16),
         vmem((spaces, zrows, quarter), BF16),
-        vmem((spaces, 128 // spaces, quarter), F32), vmem((spaces, 128 // spaces, quarter), F32),
         vmem((members, spaces, zrows, quarter), BF16),
-        vmem((members, spaces, 128 // spaces, quarter), F32),
     ]
     dma = pltpu.SemaphoreType.DMA
-    scratch += [dma((spaces,))] * 4
+    scratch += [dma((len(operands),))]
+    scratch += [dma((spaces,))] * 10
+    scratch += [dma((members,))] * 8
     scratch += [dma((members, CHUNKS))] * 2
-    scratch += [dma((members,))] * 2
-    scratch += [dma((spaces,))] * 2
-    scratch += [dma((members,))] * 6
-    scratch += [dma((spaces,))] * 8
-    scratch += [dma((members,))] * 4
+    scratch += [dma((members, spaces))] * 2
     whole = pl.BlockSpec(memory_space=pltpu.VMEM)
-    pred, loss, gout, gmsg = pl.pallas_call(
+    hbm = pl.BlockSpec(memory_space=HBM)
+    smem = pl.BlockSpec(memory_space=pltpu.SMEM)
+    shapes = (
+        jax.ShapeDtypeStruct((1, varn, grid), BF16),
+        jax.ShapeDtypeStruct((1,), F32),
+        jax.ShapeDtypeStruct((varn, latent), F32),
+        jax.ShapeDtypeStruct((latent, latent), BF16),
+    )
+    results = pl.pallas_call(
         functools.partial(step_kernel, spaces, members),
-        out_shape=(
-            jax.ShapeDtypeStruct((1, varn, grid), BF16),
-            jax.ShapeDtypeStruct((1,), F32),
-            jax.ShapeDtypeStruct((latent, varn), F32),
-            jax.ShapeDtypeStruct((latent, latent), BF16),
-        ),
-        in_specs=[whole] * 16,
-        out_specs=(whole, pl.BlockSpec(memory_space=pltpu.SMEM), whole, whole),
+        out_shape=shapes,
+        in_specs=[hbm] * len(operands),
+        out_specs=(whole, smem, whole, whole),
         scratch_shapes=scratch,
         compiler_params=pltpu.CompilerParams(
-            collective_id=0, has_side_effects=True, vmem_limit_bytes=50 * 1024 * 1024
+            collective_id=0, has_side_effects=True, vmem_limit_bytes=64 * 1024 * 1024
         ),
-    )(
-        starting_states, observed, mesh_feat, enc_send, enc_edges, dec_send, dec_edges,
-        dec_edges.T, w_in, w_src, w_dst, w_enc, w_msg, w_self, w_hid, decoder_variable_matrix.T,
-    )
-    return pred, loss, gout, gmsg
+    )(*operands)
+    pred, loss, gout, gmsg = pl.pallas_call(
+        copy_kernel,
+        out_shape=shapes,
+        in_specs=(ANY, smem, ANY, ANY),
+        out_specs=(hbm, smem, hbm, hbm),
+        scratch_shapes=[dma((3,))],
+    )(*results)
+    return pred, loss, gout.T, gmsg
 
 
 def fits(spaces, members, latent, ecap, dcap):
     return (
-        latent % (128 * members) == 0
+        members == 4
         and latent // members == 128
         and ecap % 128 == 0
         and dcap % 16 == 0

time: 72 us -> 86.4 us (1.20); the launches traced: 70.7 us -> 86.3 us
  Pallas kernels: 57.5 us -> 85.6 us
  local copies, waits for them, and re-layouts: 10.8 us -> 0 us
  between operations: 2.48 us -> 0.65 us
    pallas_call x0 -> x1, Pallas kernels: none -> 31.1 us  [fused(): pl.pallas_call(copy_kernel, out_shape=shapes, in_specs=(ANY, smem, ANY, A...]
    unnamed x26 -> x0, local copies, waits for them, and re-layouts: 9.96 us -> none
    pallas_call x1, Pallas kernels: 57.5 us -> 54.5 us  [fused(): pl.pallas_call(functools.partial(step_kernel, spaces, members), out_shape...]
where the time goes in v2:
time: 86.4 us; the launch traced here: 86.3 us
  Pallas kernels  85.6 us (99%)
    pallas_call x1, Pallas kernels, fused(): pl.pallas_call(functools.partial(step_kernel, spaces, members), out_shape...  54.5 us
    pallas_call x1, Pallas kernels, fused(): pl.pallas_call(copy_kernel, out_shape=shapes, in_specs=(ANY, smem, ANY, A...  31.1 us

profile of v2, /device:TPU:0, one launch (start us, length us, event | category | flops | bytes accessed | tf_op | source)
XLA Modules:
  0.0 86.3 jit_solution(17402916475661718689)
XLA Ops:
  0.6 54.5 %shard_map.174 = (bf16[1,100,1024]{2,1,0:T(8,128)(2,1)}, f32[1]{0:T(128)}, f32[100,512]{1,0:T(8,128)}, bf16[512,512]{1,0:T(8,128)(2,1)}) custom-call(bf16[1,100,1024]{2,1,0:T(8,128)(2,1)} %x_hbm.1, bf16[100,1024]{1,0:T(8,128)(2,1)} %obs_hbm.1, bf16[128,512]{1,0:T(8,128)(2,1)} %feat_hbm.1, s32[1,4,128]{2,1,0:T(4,128)} %esend_hbm.1, s32[16,128]{1,0:T(8,128)} %bitcast.6, ...), custom_call_target="tpu_custom_call" | custom-call | tf_op jit(solution)/shard_map/pallas_call | solution.py:429
  55.2 31.1 %shard_map.175 = (bf16[1,100,1024]{2,1,0:T(8,128)(2,1)}, f32[1]{0:T(128)}, f32[100,512]{1,0:T(8,128)}, bf16[512,512]{1,0:T(8,128)(2,1)}) custom-call(bf16[1,100,1024]{2,1,0:T(8,128)(2,1)} %get-tuple-element.12.a, f32[1]{0:T(128)} %get-tuple-element.13.b, f32[100,512]{1,0:T(8,128)} %get-tuple-element.14.c, bf16[512,512]{1,0:T(8,128)(2,1)} %get-tuple-element.15.d), custom_call_target="tpu_custom_call" | custom-call | tf_op jit(solution)/shard_map/pallas_call | solution.py:439

commit v3 on v2

--- a/solution.py
+++ b/solution.py
@@ -358,16 +358,18 @@
         gout_ref[:, cols] = block[:, zrows:, :].reshape(128, quarter)[0:varn, :].astype(F32)
 
 
-def copy_kernel(a, b, c, d, a_out, b_out, c_out, d_out, sem):
-    copies = [
-        pltpu.make_async_copy(x, y, sem.at[i])
-        for i, (x, y) in enumerate(((a, a_out), (c, c_out), (d, d_out)))
-    ]
-    for copy in copies:
-        copy.start()
+def copy_kernel(a, b, c, d, a_out, b_out, c_out, d_out, a_buf, c_buf, d_buf, sem):
+    legs = []
+    for i, (x, buf, y) in enumerate(((a, a_buf, a_out), (c, c_buf, c_out), (d, d_buf, d_out))):
+        inward = pltpu.make_async_copy(x, buf, sem.at[0, i])
+        inward.start()
+        legs.append((inward, pltpu.make_async_copy(buf, y, sem.at[1, i])))
     b_out[0] = b[0]
-    for copy in copies:
-        copy.wait()
+    for inward, outward in legs:
+        inward.wait()
+        outward.start()
+    for _, outward in legs:
+        outward.wait()
 
 
 def fused(
@@ -441,7 +443,11 @@
         out_shape=shapes,
         in_specs=(ANY, smem, ANY, ANY),
         out_specs=(hbm, smem, hbm, hbm),
-        scratch_shapes=[dma((3,))],
+        scratch_shapes=[
+            vmem(shapes[0].shape, BF16), vmem(shapes[2].shape, F32), vmem(shapes[3].shape, BF16),
+            dma((2, 3)),
+        ],
+        compiler_params=pltpu.CompilerParams(vmem_limit_bytes=64 * 1024 * 1024),
     )(*results)
     return pred, loss, gout.T, gmsg
 

time: 86.4 us -> 58.6 us (0.68)
  Pallas kernels: 85.6 us -> 57.8 us
    pallas_call x1, Pallas kernels: 31.1 us -> 3.29 us  [fused(): pl.pallas_call(copy_kernel, out_shape=shapes, in_specs=(ANY, smem, ANY, A...]
where the time goes in v3:
time: 58.6 us; the launch traced here: 58.5 us
  Pallas kernels  57.8 us (99%)
  between operations  0.65 us (1%)
    pallas_call x1, Pallas kernels, fused(): pl.pallas_call(functools.partial(step_kernel, spaces, members), out_shape...  54.5 us
    pallas_call x1, Pallas kernels, fused(): pl.pallas_call(copy_kernel, out_shape=shapes, in_specs=(ANY, smem, ANY, A...  3.29 us

profile of v3, /device:TPU:0, one launch (start us, length us, event | category | flops | bytes accessed | tf_op | source)
XLA Modules:
  0.0 58.5 jit_solution(10800172377285250674)
XLA Ops:
  0.6 54.5 %shard_map.174 = (bf16[1,100,1024]{2,1,0:T(8,128)(2,1)}, f32[1]{0:T(128)}, f32[100,512]{1,0:T(8,128)}, bf16[512,512]{1,0:T(8,128)(2,1)}) custom-call(bf16[1,100,1024]{2,1,0:T(8,128)(2,1)} %x_hbm.1, bf16[100,1024]{1,0:T(8,128)(2,1)} %obs_hbm.1, bf16[128,512]{1,0:T(8,128)(2,1)} %feat_hbm.1, s32[1,4,128]{2,1,0:T(4,128)} %esend_hbm.1, s32[16,128]{1,0:T(8,128)} %bitcast.6, ...), custom_call_target="tpu_custom_call" | custom-call | tf_op jit(solution)/shard_map/pallas_call | solution.py:431
  55.2 3.3 %shard_map.175 = (bf16[1,100,1024]{2,1,0:T(8,128)(2,1)}, f32[1]{0:T(128)}, f32[100,512]{1,0:T(8,128)}, bf16[512,512]{1,0:T(8,128)(2,1)}) custom-call(bf16[1,100,1024]{2,1,0:T(8,128)(2,1)} %get-tuple-element.12.a, f32[1]{0:T(128)} %get-tuple-element.13.b, f32[100,512]{1,0:T(8,128)} %get-tuple-element.14.c, bf16[512,512]{1,0:T(8,128)(2,1)} %get-tuple-element.15.d), custom_call_target="tpu_custom_call" | custom-call | tf_op jit(solution)/shard_map/pallas_call | solution.py:441

commit v4 on v3

--- a/solution.py
+++ b/solution.py
@@ -245,8 +245,6 @@
     drows = lax.broadcasted_iota(jnp.int32, (dslots, grid), 0)
     for k in range(k_dec):
         dhot_t[k] = one_hot(drows == dedges[k:k + 1, :])
-    a_far.wait()
-    a_passed = to_mem(aall.at[2], aall.at[3], a_ss.at[3], a_rs.at[3], 1)
     for copy in ss:
         copy.wait()
     tot = st[...]
@@ -279,6 +277,9 @@
     for j in range(1, members):
         os_.append(to_mem(gos.at[partner[j]], gor.at[j], o_ss.at[j], o_rs.at[j], j))
         ls.append(to_mem(loss_s, loss_r.at[j], l_ss.at[j], l_rs.at[j], j))
+
+    a_far.wait()
+    a_passed = to_mem(aall.at[2], aall.at[3], a_ss.at[3], a_rs.at[3], 1)
 
     mgrad = jnp.zeros((dslots, latent), F32)
     for c in range(CHUNKS):

time: 58.6 us -> 58.6 us (level)
  no operation moved by 1% of the time
where the time goes in v4:
time: 58.6 us; the launch traced here: 58.4 us
  Pallas kernels  57.8 us (99%)
  between operations  0.65 us (1%)
    pallas_call x1, Pallas kernels, fused(): pl.pallas_call(functools.partial(step_kernel, spaces, members), out_shape...  54.5 us
    pallas_call x1, Pallas kernels, fused(): pl.pallas_call(copy_kernel, out_shape=shapes, in_specs=(ANY, smem, ANY, A...  3.29 us

profile of v4, /device:TPU:0, one launch (start us, length us, event | category | flops | bytes accessed | tf_op | source)
XLA Modules:
  0.0 58.4 jit_solution(16544362080451031563)
XLA Ops:
  0.6 54.5 %shard_map.174 = (bf16[1,100,1024]{2,1,0:T(8,128)(2,1)}, f32[1]{0:T(128)}, f32[100,512]{1,0:T(8,128)}, bf16[512,512]{1,0:T(8,128)(2,1)}) custom-call(bf16[1,100,1024]{2,1,0:T(8,128)(2,1)} %x_hbm.1, bf16[100,1024]{1,0:T(8,128)(2,1)} %obs_hbm.1, bf16[128,512]{1,0:T(8,128)(2,1)} %feat_hbm.1, s32[1,4,128]{2,1,0:T(4,128)} %esend_hbm.1, s32[16,128]{1,0:T(8,128)} %bitcast.6, ...), custom_call_target="tpu_custom_call" | custom-call | tf_op jit(solution)/shard_map/pallas_call | solution.py:432
  55.1 3.3 %shard_map.175 = (bf16[1,100,1024]{2,1,0:T(8,128)(2,1)}, f32[1]{0:T(128)}, f32[100,512]{1,0:T(8,128)}, bf16[512,512]{1,0:T(8,128)(2,1)}) custom-call(bf16[1,100,1024]{2,1,0:T(8,128)(2,1)} %get-tuple-element.12.a, f32[1]{0:T(128)} %get-tuple-element.13.b, f32[100,512]{1,0:T(8,128)} %get-tuple-element.14.c, bf16[512,512]{1,0:T(8,128)(2,1)} %get-tuple-element.15.d), custom_call_target="tpu_custom_call" | custom-call | tf_op jit(solution)/shard_map/pallas_call | solution.py:442
